TPU v7x, 128 devices: a whole 4x4x4 slice. The times are simulated.
128 devices in a mesh: dom: 16 (over z, x), work: 8 (over y, core).
Axes of the slice: x: 4, y: 4, z: 4, core: 2. Of those that a mesh axis runs over, the one named last changes fastest.
Arguments:
- entity_rows: float32 [16384, 512], P(('dom', 'work')), may hold values from -1.2 to 1.2
- adagrad_state: float32 [16384], P(('dom', 'work')), may hold values from 0.005 to 0.05
- relations: float32 [4096, 512], replicated, may hold values from -6 to 6
- hub_part: int32 [1], replicated, may hold values from 0 to 15
- requests: int32 [128, 512], P(('dom', 'work')), may hold values from 0 to 127, as said below
- source_slot: int32 [256, 1024], P(('dom', 'work')), may hold values from 0 to 1535
- relation_ids: int32 [256, 1024], P(('dom', 'work')), may hold values from 0 to 4095
- target_slot: int32 [256, 1024], P(('dom', 'work')), may hold values from 0 to 1535
- negative_slot: int32 [256, 2, 1024], P(('dom', 'work')), may hold values from 0 to 1535
Outputs:
- new_rows: float32 [16384, 512], P(('dom', 'work'))
- new_state: float32 [16384], P(('dom', 'work'))
Inputs may be any that keep to these rules, and one draw needn't show every extreme that they name: The 4 rows that one device requests from one owner are distinct.
All inputs are finite; a program needn't handle non-finite values.
Results may differ from a plain program's by a relative error of at most 0.0003.
Values sent between devices are 32-bit elements; how exact they have to be, the bound alone decides.
A program may use at most 128 MiB of HBM per device.

v0:
```python
import jax
import jax.numpy as jnp
from jax import lax
from jax.sharding import PartitionSpec as P


def from_root(shard, axis, root):
    mine = lax.axis_index(axis) == root
    return lax.psum(jnp.where(mine, shard, jnp.zeros_like(shard)), axis)


def bucket_loss(working, relations, source, relation, target, negatives):
    half_width = working.shape[1] // 2
    head_rows = working[source]
    tail_rows = working[target]
    rel_rows = relations[relation]
    head_re, head_im = (head_rows[:, :half_width], head_rows[:, half_width:])
    tail_re, tail_im = (tail_rows[:, :half_width], tail_rows[:, half_width:])
    rel_re, rel_im = (rel_rows[:, :half_width], rel_rows[:, half_width:])
    query = jnp.concatenate(
        [head_re * rel_re - head_im * rel_im, head_re * rel_im + head_im * rel_re], axis=1
    )
    mirror = jnp.concatenate(
        [rel_re * tail_re + rel_im * tail_im, rel_re * tail_im - rel_im * tail_re], axis=1
    )
    positive = jnp.sum(query * tail_rows, axis=1)
    tail_scores = jnp.einsum(
        "ed,nd->en", query, working[negatives[1]], precision=lax.Precision.HIGHEST
    )
    head_scores = jnp.einsum(
        "ed,nd->en", mirror, working[negatives[0]], precision=lax.Precision.HIGHEST
    )
    neg_count = negatives.shape[1]
    return (
        jnp.sum(jax.nn.softplus(-positive))
        + (jnp.sum(jax.nn.softplus(tail_scores)) + jnp.sum(jax.nn.softplus(head_scores)))
        / neg_count
    )


def total_loss(working, relations, source, relation, target, negatives):
    totals = jnp.float32(0.0)
    for bucket in range(source.shape[0]):
        totals = totals + bucket_loss(
            working, relations, source[bucket], relation[bucket], target[bucket], negatives[bucket]
        )
    return totals


def per_device(
    entity_rows,
    adagrad_state,
    relations,
    hub_part,
    requests,
    source_slot,
    relation_ids,
    target_slot,
    negative_slot,
):
    hub_root = hub_part[0]
    dom_count = lax.axis_size("dom")
    work_count = lax.axis_size("work")
    owners = dom_count * work_count
    row_count = entity_rows.shape[0]
    width = entity_rows.shape[1]
    capacity = requests.shape[1] // owners
    hub_piece = from_root(entity_rows, "dom", hub_root)
    hub_block = lax.all_gather(hub_piece, "work", axis=0, tiled=True)
    request_rows = requests.reshape(owners, capacity)
    wanted = lax.all_to_all(request_rows, ("dom", "work"), split_axis=0, concat_axis=0, tiled=True)
    fetched = lax.all_to_all(
        entity_rows[wanted], ("dom", "work"), split_axis=0, concat_axis=0, tiled=True
    )
    working = jnp.concatenate([hub_block, fetched.reshape(-1, width)], axis=0)
    gradient = jax.grad(total_loss)(
        working, relations, source_slot, relation_ids, target_slot, negative_slot
    )
    hub_count = hub_block.shape[0]
    far_grad = gradient[hub_count:].reshape(fetched.shape)
    returned = lax.all_to_all(far_grad, ("dom", "work"), split_axis=0, concat_axis=0, tiled=True)
    collected = jnp.zeros_like(entity_rows).at[wanted.reshape(-1)].add(returned.reshape(-1, width))
    hub_grad = gradient[:hub_count]
    hub_total = lax.psum(hub_grad, ("dom", "work"))
    own_share = lax.dynamic_slice_in_dim(
        hub_total, lax.axis_index("work") * row_count, row_count, 0
    )
    is_owner = lax.axis_index("dom") == hub_root
    collected = collected + jnp.where(is_owner, own_share, jnp.zeros_like(own_share))
    new_state = adagrad_state + jnp.mean(collected * collected, axis=1)
    new_rows = entity_rows - 0.1 * collected / (jnp.sqrt(new_state)[:, None] + 1e-10)
    return (new_rows, new_state)


def solution(mesh):
    return jax.shard_map(
        per_device,
        mesh=mesh,
        in_specs=(
            P(("dom", "work"), None),
            P(("dom", "work")),
            P(),
            P(),
            P(("dom", "work"), None),
            P(("dom", "work"), None),
            P(("dom", "work"), None),
            P(("dom", "work"), None),
            P(("dom", "work"), None, None),
        ),
        out_specs=(P(("dom", "work"), None), P(("dom", "work"))),
        check_vma=False,
    )
```

profile of v0, /device:TPU:1, one launch (start us, length us, event | category | flops | bytes accessed | tf_op | source)
XLA Modules:
  0.0 598.9 jit_solution(4531551215260391825)
XLA Ops:
  8.7 89.4 %all-reduce.11.cloned.1.call-done = f32[128,512]{1,0:T(8,128)} async-done(((f32[128,512]{1,0:T(8,128)}), f32[128,512]{1,0:T(8,128)}) %all-reduce.11.cloned.1.call-update) | async-done | bytes 262160 | tf_op jit(solution)/shard_map/psum | solution.py:9
  100.7 8.9 %all-to-all-start = ((s32[128,1,4]{2,1,0:T(1,128)}), s32[128,1,4]{2,1,0:T(1,128)S(1)}, u32[]{:S(2)}, u32[]{:S(2)}) async-start(s32[128,1,4]{2,1,0:T(1,128)} %bitcast.5), calls=%async_computation | async-start | bytes 131072 | tf_op jit(solution)/shard_map/all_to_all | solution.py:71
  112.0 8.6 %gather_fusion.6 = f32[1024,512]{1,0:T(8,128)} fusion(f32[4096,512]{1,0:T(8,128)} %param.11, s32[1024]{0:T(1024)S(1)} %get-tuple-element.46), kind=kCustom, calls=%fused_computation.6 | custom fusion | bytes 4198400 | tf_op jit(solution)/shard_map/jvp()/gather | solution.py:16
  120.6 8.8 %gather_fusion = f32[1024,512]{1,0:T(8,128)} fusion(f32[4096,512]{1,0:T(8,128)} %param.11, s32[1024]{0:T(1024)S(1)} %get-tuple-element.47), kind=kCustom, calls=%fused_computation | custom fusion | bytes 4198400 | tf_op jit(solution)/shard_map/jvp()/gather | solution.py:16
  132.5 9.8 %all-to-all-start.1 = ((f32[128,4,512]{2,1,0:T(4,128)}), f32[128,4,512]{2,1,0:T(4,128)S(1)}, u32[]{:S(2)}, u32[]{:S(2)}) async-start(f32[128,4,512]{2,1,0:T(4,128)} %reshape.380), calls=%async_computation.1 | async-start | bytes 2097152 | tf_op jit(solution)/shard_map/all_to_all | solution.py:72
  142.5 18.8 %all-to-all-done.1 = f32[128,4,512]{2,1,0:T(4,128)S(1)} async-done(((f32[128,4,512]{2,1,0:T(4,128)}), f32[128,4,512]{2,1,0:T(4,128)S(1)}, u32[]{:S(2)}, u32[]{:S(2)}) %all-to-all-start.1) | async-done | bytes 1048608 | tf_op jit(solution)/shard_map/all_to_all | solution.py:72
  184.2 10.1 %fusion.8 = f32[1024,1024]{1,0:T(8,128)S(1)} fusion(f32[1024,512]{1,0:T(8,128)S(1)} %copy-done.14, f32[1024,256]{1,0:T(8,128)S(1)} %get-tuple-element.22, f32[1024,256]{1,0:T(8,128)S(1)} %get-tuple-element.23), kind=kOutput, calls=%fused_computation.40 | convolution fusion | flops 6455558144 | bytes 8388608 | tf_op jit(solution)/shard_map/jvp(ed,nd->en)/dot_general | solution.py:30
  194.3 8.6 %fusion.61 = f32[1024,512]{1,0:T(8,128)} fusion(f32[1024,1024]{1,0:T(8,128)S(1)} %fusion.8, f32[1024,512]{1,0:T(8,128)S(1)} %copy-done.14), kind=kOutput, calls=%fused_computation.154 | convolution fusion | flops 6442450944 | bytes 8388608 | tf_op jit(solution)/shard_map/transpose(jvp(ed,nd->en))/dot_general | solution.py:30
  230.5 10.1 %fusion.2 = f32[1024,1024]{1,0:T(8,128)S(1)} fusion(f32[1024,512]{1,0:T(8,128)S(1)} %copy-done.15, f32[1024,256]{1,0:T(8,128)S(1)} %get-tuple-element.26, f32[1024,256]{1,0:T(8,128)S(1)} %get-tuple-element.27), kind=kOutput, calls=%fused_computation.34 | convolution fusion | flops 6455558144 | bytes 8388608 | tf_op jit(solution)/shard_map/jvp(ed,nd->en)/dot_general | solution.py:30
  240.5 8.2 %fusion.60 = f32[1024,512]{1,0:T(8,128)} fusion(f32[1024,1024]{1,0:T(8,128)S(1)} %fusion.2, f32[1024,512]{1,0:T(8,128)S(1)} %copy-done.15), kind=kOutput, calls=%fused_computation.153 | convolution fusion | flops 6442450944 | bytes 8388608 | tf_op jit(solution)/shard_map/transpose(jvp(ed,nd->en))/dot_general | solution.py:30
  248.8 8.2 %fusion.33 = f32[1024,512]{1,0:T(8,128)} fusion(f32[1024,1024]{1,0:T(8,128)S(1)} %fusion.2, f32[1024,256]{1,0:T(8,128)S(1)} %get-tuple-element.26, f32[1024,256]{1,0:T(8,128)S(1)} %get-tuple-element.27), kind=kOutput, calls=%fused_computation.73 | convolution fusion | flops 6442975232 | bytes 8388608 | tf_op jit(solution)/shard_map/transpose(jvp(ed,nd->en))/dot_general | solution.py:30
  272.2 10.1 %fusion.11 = f32[1024,1024]{1,0:T(8,128)S(1)} fusion(f32[1024,512]{1,0:T(8,128)S(1)} %copy-done.13, f32[1024,256]{1,0:T(8,128)S(1)} %copy-done.6, f32[1024,256]{1,0:T(8,128)S(1)} %copy-done.5), kind=kOutput, calls=%fused_computation.43 | convolution fusion | flops 6455558144 | bytes 8388608 | tf_op jit(solution)/shard_map/jvp(ed,nd->en)/dot_general | solution.py:27
  297.4 8.4 %scatter_custom_fusion.5 = f32[1536,512]{1,0:T(8,128)} fusion(s32[1024]{0:T(1024)S(1)} %bitcast.71, f32[1024,512]{1,0:T(8,128)S(1)} %fusion.44, f32[]{:T(128)} %constant.18.clone.1), kind=kCustom, calls=%fused_computation.75 | custom fusion | flops 524288 | bytes 3145732 | tf_op jit(solution)/shard_map/transpose(jvp())/scatter-add | solution.py:28
  305.8 9.5 %scatter_custom_fusion = f32[1536,512]{1,0:T(8,128)} fusion(s32[1024]{0:T(1024)S(1)} %bitcast.69, f32[1024,512]{1,0:T(8,128)} %fusion.33, f32[]{:T(128)} %constant.18.clone.1), kind=kCustom, calls=%fused_computation.80 | custom fusion | flops 524288 | bytes 3146240 | tf_op jit(solution)/shard_map/transpose(jvp())/scatter-add | solution.py:31
  315.4 11.6 %fusion.5 = f32[1024,1024]{1,0:T(8,128)S(1)} fusion(f32[1024,512]{1,0:T(8,128)} %gather_fusion.5, f32[1024,256]{1,0:T(8,128)S(1)} %copy-done.8, f32[1024,256]{1,0:T(8,128)S(1)} %copy-done.7), kind=kOutput, calls=%fused_computation.37 | convolution fusion | flops 6455558144 | bytes 8388608 | tf_op jit(solution)/shard_map/jvp(ed,nd->en)/dot_general | solution.py:27
  327.1 8.4 %fusion.45 = f32[1024,512]{1,0:T(8,128)} fusion(f32[1024,1024]{1,0:T(8,128)S(1)} %fusion.5, f32[1024,256]{1,0:T(8,128)S(1)} %copy-done.8, f32[1024,256]{1,0:T(8,128)S(1)} %copy-done.7), kind=kOutput, calls=%fused_computation.101 | convolution fusion | flops 6442975232 | bytes 8388608 | tf_op jit(solution)/shard_map/transpose(jvp(ed,nd->en))/dot_general | solution.py:27
  343.6 9.5 %scatter_custom_fusion.1 = f32[1536,512]{1,0:T(8,128)} fusion(s32[1024]{0:T(1024)S(1)} %bitcast.67, f32[1024,512]{1,0:T(8,128)} %fusion.45, f32[]{:T(128)} %constant.18.clone.1), kind=kCustom, calls=%fused_computation.78 | custom fusion | flops 524288 | bytes 3146240 | tf_op jit(solution)/shard_map/transpose(jvp())/scatter-add | solution.py:28
  357.7 9.3 %scatter_custom_fusion.7 = f32[1536,512]{1,0:T(8,128)} fusion(s32[1024]{0:T(1024)S(1)} %bitcast.59, f32[1024,256]{1,0:T(8,128)} %get-tuple-element.5, f32[]{:T(128)} %constant.18.clone.1, f32[1024,256]{1,0:T(8,128)} %get-tuple-element.4), kind=kCustom, calls=%fused_computation.48 | custom fusion | flops 1048576 | bytes 5243904 | tf_op jit(solution)/shard_map/transpose(jvp())/scatter-add | solution.py:14
  371.5 9.6 %scatter_custom_fusion.3 = f32[1536,512]{1,0:T(8,128)} fusion(s32[1024]{0:T(1024)S(1)} %bitcast.57, f32[1024,256]{1,0:T(8,128)} %get-tuple-element.13, f32[]{:T(128)} %constant.18.clone.1, f32[1024,256]{1,0:T(8,128)} %get-tuple-element.12), kind=kCustom, calls=%fused_computation.60 | custom fusion | flops 1048576 | bytes 5243904 | tf_op jit(solution)/shard_map/transpose(jvp())/scatter-add | solution.py:14
  386.6 11.4 %scatter_custom_fusion.2 = f32[1536,512]{1,0:T(8,128)} fusion(f32[1536,512]{1,0:T(8,128)} %add_any.63, s32[1024]{0:T(1024)S(1)} %bitcast.63, f32[1024,256]{1,0:T(8,128)S(1)} %copy-done.16, f32[]{:T(128)} %constant.18.clone.1, f32[1024,256]{1,0:T(8,128)} %get-tuple-element.25, f32[1024]{0:T(1024)S(1)} %fusion.48, f32[1024,256]{1,0:T(8,128)S(1)} %copy-done.9, ...), kind=kCustom, calls=%fused_computation.65 | custom fusion | flops 2621440 | bytes 7345152 | tf_op jit(solution)/shard_map/transpose(jvp())/scatter-add | solution.py:15
  401.6 8.4 %scatter_fusion = f32[1536,512]{1,0:T(8,128)S(1)} fusion(f32[1536,512]{1,0:T(8,128)S(1)} %add_any.72, s32[1024]{0:T(1024)S(1)} %bitcast.55, f32[1024,512]{1,0:T(8,128)} %fusion.32), kind=kCustom, calls=%fused_computation.15 | custom fusion | flops 524288 | bytes 6295552 | tf_op jit(solution)/shard_map/transpose(jvp())/scatter-add | solution.py:31
  414.3 11.9 %scatter_custom_fusion.6 = f32[1536,512]{1,0:T(8,128)} fusion(f32[1536,512]{1,0:T(8,128)} %add_any.73, s32[1024]{0:T(1024)S(1)} %bitcast.61, f32[1024,256]{1,0:T(8,128)} %get-tuple-element.20, f32[]{:T(128)} %constant.18.clone.1, f32[1024,256]{1,0:T(8,128)} %get-tuple-element.21, f32[1024]{0:T(1024)S(1)} %fusion.51, f32[1024,256]{1,0:T(8,128)} %get-tuple-element.9, ...), kind=kCustom, calls=%fused_computation.53 | custom fusion | flops 2621440 | bytes 7345152 | tf_op jit(solution)/shard_map/transpose(jvp())/scatter-add | solution.py:15
  440.1 19.5 %all-to-all-done.2 = f32[128,4,512]{2,1,0:T(4,128)S(1)} async-done(((f32[128,4,512]{2,1,0:T(4,128)}), f32[128,4,512]{2,1,0:T(4,128)S(1)}, u32[]{:S(2)}, u32[]{:S(2)}) %all-to-all-start.2) | async-done | bytes 1048608 | tf_op jit(solution)/shard_map/all_to_all | solution.py:81
  460.0 126.1 %all-reduce.13.cloned.1.call-done = f32[1024,512]{1,0:T(8,128)} async-done(((f32[1024,512]{1,0:T(8,128)}), f32[1024,512]{1,0:T(8,128)}) %all-reduce.13.cloned.1.call-update) | async-done | bytes 2097168 | tf_op jit(solution)/shard_map/psum | solution.py:84
  (107 shorter events, 140.8 us)
Async XLA Ops:
  7.2 90.9 %all-reduce.11.cloned.1.call-start = ((), (), s32[]{:S(2)}) async-start(), calls=%async_computation.3 | async-start | bytes 524288 | tf_op jit(solution)/shard_map/psum | solution.py:9
  8.6 153.9 %all-gather.2.cloned.1.call-start = ((), (), s32[]{:S(2)}) async-start(), calls=%async_computation.4 | async-start | bytes 2359296 | tf_op jit(solution)/shard_map/all_gather | solution.py:69
  100.7 28.7 %all-to-all-start = ((s32[128,1,4]{2,1,0:T(1,128)}), s32[128,1,4]{2,1,0:T(1,128)S(1)}, u32[]{:S(2)}, u32[]{:S(2)}) async-start(s32[128,1,4]{2,1,0:T(1,128)} %bitcast.5), calls=%async_computation | async-start | bytes 131072 | tf_op jit(solution)/shard_map/all_to_all | solution.py:71
  120.6 8.9 %copy-start = (f32[128,512]{1,0:T(8,128)S(1)}, f32[128,512]{1,0:T(8,128)}, u32[]{:S(2)}) copy-start(f32[128,512]{1,0:T(8,128)} %param.9) | copy-start | bytes 786436
  131.2 11.2 %copy-start.18 = (s32[2,1024]{1,0:T(2,128)S(1)}, s32[2,1024]{1,0:T(2,128)}, u32[]{:S(2)}) copy-start(s32[2,1024]{1,0:T(2,128)} %param.16) | copy-start | bytes 24580
  132.5 28.7 %all-to-all-start.1 = ((f32[128,4,512]{2,1,0:T(4,128)}), f32[128,4,512]{2,1,0:T(4,128)S(1)}, u32[]{:S(2)}, u32[]{:S(2)}) async-start(f32[128,4,512]{2,1,0:T(4,128)} %reshape.380), calls=%async_computation.1 | async-start | bytes 2097152 | tf_op jit(solution)/shard_map/all_to_all | solution.py:72
  142.3 443.8 %all-reduce.13.cloned.1.call-start = ((), (), s32[]{:S(2)}) async-start(), calls=%async_computation.5 | async-start | bytes 4194304 | tf_op jit(solution)/shard_map/psum | solution.py:84
  162.6 1.9 copy-start.17
  179.5 4.7 copy-start.14
  225.8 4.7 copy-start.15
  267.2 2.9 copy-start.1
  267.2 3.1 copy-start.5
  267.2 3.4 copy-start.6
  305.8 9.5 %copy-start.7 = (f32[1024,256]{1,0:T(8,128)S(1)}, f32[1024,256]{1,0:T(8,128)}, u32[]{:S(2)}) copy-start(f32[1024,256]{1,0:T(8,128)} %get-tuple-element.16) | copy-start | bytes 3145732
  305.8 9.5 %copy-start.8 = (f32[1024,256]{1,0:T(8,128)S(1)}, f32[1024,256]{1,0:T(8,128)}, u32[]{:S(2)}) copy-start(f32[1024,256]{1,0:T(8,128)} %get-tuple-element.17) | copy-start | bytes 3145732
  327.0 8.4 %copy-start.2 = (f32[1024,512]{1,0:T(8,128)S(1)}, f32[1024,512]{1,0:T(8,128)}, u32[]{:S(2)}) copy-start(f32[1024,512]{1,0:T(8,128)} %gather_fusion.2) | copy-start | bytes 6291460
  327.0 8.4 %copy-start.12 = (f32[1024,512]{1,0:T(8,128)S(1)}, f32[1024,512]{1,0:T(8,128)}, u32[]{:S(2)}) copy-start(f32[1024,512]{1,0:T(8,128)} %gather_fusion.5) | copy-start | bytes 6291460
  343.6 9.5 %copy-start.4 = (f32[1024,512]{1,0:T(8,128)S(1)}, f32[1024,512]{1,0:T(8,128)}, u32[]{:S(2)}) copy-start(f32[1024,512]{1,0:T(8,128)} %gather_fusion.6) | copy-start | bytes 6291460
  357.7 9.3 %copy-start.3 = (f32[1024,512]{1,0:T(8,128)S(1)}, f32[1024,512]{1,0:T(8,128)}, u32[]{:S(2)}) copy-start(f32[1024,512]{1,0:T(8,128)} %gather_fusion) | copy-start | bytes 6291460
  381.1 5.5 copy-start.9
  381.1 5.5 copy-start.16
  414.3 11.9 %copy-start.10 = (f32[1536,512]{1,0:T(8,128)S(1)}, f32[1536,512]{1,0:T(8,128)}, u32[]{:S(2)}) copy-start(f32[1536,512]{1,0:T(8,128)} %scatter_custom_fusion.7) | copy-start | bytes 9437188
  434.5 25.1 %all-to-all-start.2 = ((f32[128,4,512]{2,1,0:T(4,128)}), f32[128,4,512]{2,1,0:T(4,128)S(1)}, u32[]{:S(2)}, u32[]{:S(2)}) async-start(f32[128,4,512]{2,1,0:T(4,128)} %reshape.369), calls=%async_computation.2 | async-start | bytes 2097152 | tf_op jit(solution)/shard_map/all_to_all | solution.py:81
  587.1 3.8 copy-start.19
  (3 other events, 4.5 us)
Sparse Core Ops, SparseCore 0:
  11.7 86.3 all-reduce.10
  99.9 26.6 all-gather.1
  432.2 153.8 all-reduce.12
where the time goes:
time: 604 us; the launch traced here: 599 us
  waiting for transfers between devices  254 us (42%)
  other arithmetic  127 us (21%)
  matrix products  107 us (18%)
  local copies, waits for them, and re-layouts  73.2 us (12%)
  starting transfers between devices  23.5 us (4%)
  between operations  15 us (2%)
    psum x1, waiting for transfers between devices, per_device(): hub_total = lax.psum(hub_grad, ('dom', 'work'))  126 us
    psum x1, waiting for transfers between devices, from_root(): return lax.psum(jnp.where(mine, shard, jnp.zeros_like(shard)), axis)  89.4 us
    dot_general x6, matrix products, bucket_loss(): jnp.einsum('ed,nd->en', query, working[negatives[1]], precision=lax.Preci...  53.4 us
    dot_general x6, matrix products, bucket_loss(): jnp.einsum('ed,nd->en', mirror, working[negatives[0]], precision=lax.Prec...  53.2 us
    scatter-add x2, other arithmetic, bucket_loss(): tail_rows = working[target]  23.3 us
    all_to_all x1, waiting for transfers between devices, per_device(): lax.all_to_all(far_grad, ('dom', 'work'), split_axis=0, concat_axis=0, ti...  19.5 us
    scatter-add x2, other arithmetic, bucket_loss(): head_rows = working[source]  18.9 us
    all_to_all x1, waiting for transfers between devices, per_device(): lax.all_to_all(entity_rows[wanted], ('dom', 'work'), split_axis=0, concat...  18.8 us
  transfers between devices with their start and end apart: 6, of which 4 were waited for; matrix products, arithmetic and copies ran while one was open for 5% of the time, Pallas kernels for 0%

commit v1 on v0

v1 whole, which is shorter than its diff:
```python
import functools
import jax
import jax.numpy as jnp
from jax import lax
from jax.experimental import pallas as pl
from jax.experimental.pallas import tpu as pltpu
from jax.sharding import PartitionSpec as P

F32 = jnp.float32
BF16 = jnp.bfloat16
NT = (((1,), (1,)), ((), ()))


def train_kernel(tiles, src_s, tgt_s, w_ref, rel_ref, src_v, tgt_v, neg_ref,
                 hub_out, far_out,
                 wb, wbt, cnt, acc, hlin, tlin, qf, rhs, lhs, rlo, dneg):
    step = pl.program_id(0)
    edges = rel_ref.shape[0]
    slots = wb.shape[0]
    hub = hub_out.shape[0]
    negs = neg_ref.shape[2]

    @pl.when(step == 0)
    def _():
        for c in range(4):
            part = w_ref[pl.ds(c, slots, stride=4), :]
            wb[:, c * 128:(c + 1) * 128] = part.astype(BF16)
            wbt[c * 128:(c + 1) * 128, :] = part.T.astype(BF16)
        acc[...] = jnp.zeros_like(acc)

    @pl.when(lax.rem(step, tiles) == 0)
    def _():
        groups = slots // 128
        high = lax.broadcasted_iota(jnp.int32, (16, negs), 0)
        low = lax.broadcasted_iota(jnp.int32, (128, negs), 0)
        for side in range(2):
            slot = neg_ref[0, side:side + 1, :]
            top = (high == lax.shift_right_logical(slot, 7)).astype(F32).astype(BF16)
            end = (low == jnp.bitwise_and(slot, 127)).astype(F32).astype(BF16)
            table = lax.dot_general(end, top, NT, preferred_element_type=F32) * (0.5 / negs)
            for g in range(groups):
                cnt[side, g * 128:(g + 1) * 128, :] = jnp.broadcast_to(table[:, g:g + 1], (128, 128))

    base = step * edges

    def gather(e, carry):
        s = src_s[base + e]
        t = tgt_s[base + e]
        hlin[pl.ds(pl.multiple_of(e * 4, 4), 4), :] = w_ref[pl.ds(pl.multiple_of(s * 4, 4), 4), :]
        tlin[pl.ds(pl.multiple_of(e * 4, 4), 4), :] = w_ref[pl.ds(pl.multiple_of(t * 4, 4), 4), :]
        return carry

    lax.fori_loop(0, edges, gather, 0, unroll=8)

    def cols(c):
        return slice(c * 128, (c + 1) * 128)

    def head(c):
        return hlin[pl.ds(c, edges, stride=4), :]

    def tail(c):
        return tlin[pl.ds(c, edges, stride=4), :]

    score = jnp.zeros((edges, 128), F32)
    for a in range(2):
        b = a + 2
        hr, hi, tr, ti = head(a), head(b), tail(a), tail(b)
        rr, ri = rel_ref[:, cols(a)], rel_ref[:, cols(b)]
        qr = hr * rr - hi * ri
        qi = hr * ri + hi * rr
        ur = rr * tr + ri * ti
        ui = rr * ti - ri * tr
        score = score + (qr * tr + qi * ti)
        qf[:, cols(a)] = qr
        qf[:, cols(b)] = qi
        rhs[0:edges, cols(a)] = qr.astype(BF16)
        rhs[0:edges, cols(b)] = qi.astype(BF16)
        rhs[edges:2 * edges, cols(a)] = ur.astype(BF16)
        rhs[edges:2 * edges, cols(b)] = ui.astype(BF16)
    positive = jnp.sum(score, axis=1, keepdims=True)
    slope = 0.5 * jnp.tanh(0.5 * positive) - 0.5

    half = slots // 2
    for side in range(2):
        mine = rhs[side * edges:(side + 1) * edges, :]
        for m in range(2):
            rows = slice(m * half, (m + 1) * half)
            st = lax.dot_general(wb[rows, :], mine, NT, preferred_element_type=F32)
            weight = cnt[1 - side, rows, :]
            weight = jnp.concatenate([weight] * (edges // 128), axis=1)
            lhs[rows, side * edges:(side + 1) * edges] = (weight * jnp.tanh(0.5 * st) + weight).astype(BF16)
        dneg[side] = jnp.dot(wbt[...], lhs[:, side * edges:(side + 1) * edges], preferred_element_type=F32)

    row = lax.broadcasted_iota(jnp.int32, (slots, edges), 0)
    lhs[:, 2 * edges:3 * edges] = (row == src_v[0]).astype(F32).astype(BF16)
    lhs[:, 3 * edges:4 * edges] = (row == tgt_v[0]).astype(F32).astype(BF16)

    def put(at, c, value):
        top = value.astype(BF16)
        rhs[(2 + at) * edges:(3 + at) * edges, cols(c)] = top
        rlo[at * edges:(at + 1) * edges, cols(c)] = (value - top.astype(F32)).astype(BF16)

    for a in range(2):
        b = a + 2
        rr, ri = rel_ref[:, cols(a)], rel_ref[:, cols(b)]
        dqr = slope * tail(a) + dneg[0, cols(a), :].T
        dqi = slope * tail(b) + dneg[0, cols(b), :].T
        put(0, a, dqr * rr + dqi * ri)
        put(0, b, dqi * rr - dqr * ri)
        dur = dneg[1, cols(a), :].T
        dui = dneg[1, cols(b), :].T
        put(1, a, slope * qf[:, cols(a)] + (dur * rr - dui * ri))
        put(1, b, slope * qf[:, cols(b)] + (dur * ri + dui * rr))

    for m in range(2):
        rows = slice(m * half, (m + 1) * half)
        acc[rows, :] += (
            jnp.dot(lhs[rows, :], rhs[...], preferred_element_type=F32)
            + jnp.dot(lhs[rows, 2 * edges:], rlo[...], preferred_element_type=F32)
        )

    @pl.when(step == pl.num_programs(0) - 1)
    def _():
        hub_out[...] = acc[0:hub, :]
        for c in range(4):
            far_out[pl.ds(c, slots - hub, stride=4), :] = acc[hub:, cols(c)]


def train(w_lin, rel_rows, source, target, negative, hub, edges=256):
    buckets, count = source.shape
    negs = negative.shape[2]
    slots = w_lin.shape[0] // 4
    width = rel_rows.shape[1]
    tiles = count // edges
    steps = buckets * tiles
    whole = lambda shape: pl.BlockSpec(shape, lambda i, *_: (0,) * len(shape))
    lane = pl.BlockSpec((1, 1, edges), lambda i, *_: (i, 0, 0))
    return pl.pallas_call(
        functools.partial(train_kernel, tiles),
        grid_spec=pltpu.PrefetchScalarGridSpec(
            num_scalar_prefetch=2,
            grid=(steps,),
            in_specs=[
                whole(w_lin.shape),
                pl.BlockSpec((edges, width), lambda i, *_: (i, 0)),
                lane,
                lane,
                pl.BlockSpec((1, 2, negs), lambda i, *_: (i // tiles, 0, 0)),
            ],
            out_specs=[whole((hub, width)), whole(((slots - hub) * 4, 128))],
            scratch_shapes=[
                pltpu.VMEM((slots, width), BF16),
                pltpu.VMEM((width, slots), BF16),
                pltpu.VMEM((2, slots, 128), F32),
                pltpu.VMEM((slots, width), F32),
                pltpu.VMEM((edges * 4, 128), F32),
                pltpu.VMEM((edges * 4, 128), F32),
                pltpu.VMEM((edges, width), F32),
                pltpu.VMEM((4 * edges, width), BF16),
                pltpu.VMEM((slots, 4 * edges), BF16),
                pltpu.VMEM((2 * edges, width), BF16),
                pltpu.VMEM((2, width, edges), F32),
            ],
        ),
        out_shape=[
            jax.ShapeDtypeStruct((hub, width), F32),
            jax.ShapeDtypeStruct(((slots - hub) * 4, 128), F32),
        ],
        compiler_params=pltpu.CompilerParams(vmem_limit_bytes=56 * 1024 * 1024),
        name="train",
    )(
        source.reshape(-1), target.reshape(-1), w_lin, rel_rows,
        source.reshape(steps, 1, edges), target.reshape(steps, 1, edges), negative,
    )


MESH = pl.DeviceIdType.MESH


def ring(at, by, size):
    return lax.rem(at + by, size)


def greet(doms, works):
    dom, work = lax.axis_index("dom"), lax.axis_index("work")
    barrier = pltpu.get_barrier_semaphore()

    def call(i, carry):
        peer = (ring(dom, i // works, doms), ring(work, lax.rem(i, works), works))
        pl.semaphore_signal(barrier, inc=1, device_id=peer, device_id_type=MESH)
        return carry

    lax.fori_loop(1, doms * works, call, 0)
    pl.semaphore_wait(barrier, doms * works - 1)


def arrived(ref, sem):
    pltpu.make_async_copy(ref, ref, sem).wait()


def fetch_kernel(doms, works, cap, ent_ref, req_ref, hub_ref, ids_ref, rel_hbm,
                 w_ref, want_ref, rel_ref,
                 elin, erow, hub1, piece, send, want_s, relv,
                 rel_sem, req_send, req_recv, loc_sem, h1_send, h1_recv, h2_send, h2_recv,
                 x_send, x_recv, far_send, far_recv):
    dom, work = lax.axis_index("dom"), lax.axis_index("work")
    me = dom * works + work
    core, line = lax.rem(work, 2), work // 2
    lines = works // 2
    count = doms * works
    own = ent_ref.shape[0]
    part = own // doms * 4
    hub = works * own
    msg = cap * 4

    load = pltpu.make_async_copy(rel_hbm, relv, rel_sem)
    load.start()
    for c in range(4):
        elin[pl.ds(c, own, stride=4), :] = ent_ref[:, c * 128:(c + 1) * 128]
        erow[:, c, :] = ent_ref[:, c * 128:(c + 1) * 128]
    greet(doms, works)

    want_ref[me] = req_ref[me]

    def ask(i, carry):
        pd, pw = ring(dom, i // works, doms), ring(work, lax.rem(i, works), works)
        pltpu.make_async_remote_copy(
            src_ref=req_ref.at[pd * works + pw], dst_ref=want_ref.at[me],
            send_sem=req_send, recv_sem=req_recv, device_id=(pd, pw), device_id_type=MESH,
        ).start()
        return carry

    lax.fori_loop(1, count, ask, 0)

    hub1[dom] = elin[pl.ds(pl.multiple_of(dom * part, part), part), :]

    def spread(i, carry):
        pd = ring(dom, i, doms)
        pltpu.make_async_remote_copy(
            src_ref=elin.at[pl.ds(pl.multiple_of(pd * part, part), part), :], dst_ref=hub1.at[dom],
            send_sem=h1_send, recv_sem=h1_recv, device_id=(pd, work), device_id_type=MESH,
        ).start()
        return carry

    lax.fori_loop(1, doms, spread, 0)
    arrived(hub1.at[pl.ds(0, doms - 1)], h1_recv)
    piece[...] = hub1[hub_ref[0]]

    def rows_of(w, d):
        return w_ref.at[pl.ds(pl.multiple_of((w * doms + d) * part, part), part), :]

    pltpu.make_async_copy(piece, rows_of(work, dom), h2_recv.at[line]).start()

    def gather(i, carry):
        pd, pw = ring(dom, i // lines, doms), ring(line, lax.rem(i, lines), lines) * 2 + core
        pltpu.make_async_remote_copy(
            src_ref=piece, dst_ref=rows_of(work, dom),
            send_sem=h2_send, recv_sem=h2_recv.at[line], device_id=(pd, pw), device_id_type=MESH,
        ).start()
        return carry

    lax.fori_loop(1, doms * lines, gather, 0)

    arrived(want_ref.at[pl.ds(0, count - 1)], req_recv)
    copy = pltpu.make_async_copy(want_ref, want_s, loc_sem)
    copy.start()
    copy.wait()

    def fill(p):
        for c in range(cap):
            send[p, c * 4:(c + 1) * 4, :] = erow[want_s[p, 0, c]]

    def far_rows(p):
        return w_ref.at[pl.ds(pl.multiple_of(hub * 4 + p * msg, msg), msg), :]

    fill(me)
    pltpu.make_async_copy(send.at[me], far_rows(me), far_recv).start()

    def answer(i, carry):
        pd, pw = ring(dom, i // works, doms), ring(work, lax.rem(i, works), works)
        p = pd * works + pw
        fill(p)
        pltpu.make_async_remote_copy(
            src_ref=send.at[p], dst_ref=far_rows(me),
            send_sem=far_send, recv_sem=far_recv, device_id=(pd, pw), device_id_type=MESH,
        ).start()
        return carry

    lax.fori_loop(1, count, answer, 0)

    load.wait()

    def pick(e, carry):
        rel_ref[e] = relv[ids_ref[e]]
        return carry

    lax.fori_loop(0, rel_ref.shape[0], pick, 0, unroll=8)

    def block(w):
        return w_ref.at[pl.ds(pl.multiple_of(w * doms * part, doms * part), doms * part), :]

    def across(y, carry):
        mine = block(y * 2 + core)
        arrived(mine, h2_recv.at[y])
        pltpu.make_async_remote_copy(
            src_ref=mine, dst_ref=mine, send_sem=x_send, recv_sem=x_recv,
            device_id=(dom, line * 2 + 1 - core), device_id_type=MESH,
        ).start()
        return carry

    lax.fori_loop(0, lines, across, 0)
    half = w_ref.at[pl.ds(0, hub * 2), :]
    arrived(half, x_recv)
    arrived(w_ref.at[pl.ds(hub * 4, count * msg), :], far_recv)
    arrived(half, x_send)
    arrived(w_ref.at[pl.ds(0, (doms * lines - 1) * part), :], h2_send)
    arrived(hub1.at[pl.ds(0, doms - 1)], h1_send)
    arrived(send.at[pl.ds(0, count - 1)], far_send)
    arrived(req_ref.at[pl.ds(0, count - 1)], req_send)


def fetch(doms, works, entity_rows, asked, hub_part, relation_ids, relations):
    own, width = entity_rows.shape
    count = doms * works
    cap = 4
    slots = works * own + count * cap
    edges = relation_ids.shape[0]
    vmem, smem = pl.BlockSpec(memory_space=pltpu.VMEM), pl.BlockSpec(memory_space=pltpu.SMEM)
    dma = pltpu.SemaphoreType.DMA
    return pl.pallas_call(
        functools.partial(fetch_kernel, doms, works, cap),
        in_specs=[vmem, vmem, smem, smem, pl.BlockSpec(memory_space=pl.ANY)],
        out_specs=[vmem, vmem, vmem],
        out_shape=[
            jax.ShapeDtypeStruct((slots * 4, 128), F32),
            jax.ShapeDtypeStruct(asked.shape, jnp.int32),
            jax.ShapeDtypeStruct((edges, width), F32),
        ],
        scratch_shapes=[
            pltpu.VMEM((own * 4, 128), F32),
            pltpu.VMEM((own, 4, 128), F32),
            pltpu.VMEM((doms, own // doms * 4, 128), F32),
            pltpu.VMEM((own // doms * 4, 128), F32),
            pltpu.VMEM((count, cap * 4, 128), F32),
            pltpu.SMEM(asked.shape, jnp.int32),
            pltpu.VMEM(relations.shape, F32),
            dma, dma, dma, dma, dma, dma, dma, dma((works // 2,)), dma, dma, dma, dma,
        ],
        compiler_params=pltpu.CompilerParams(
            collective_id=0, has_side_effects=True, vmem_limit_bytes=48 * 1024 * 1024
        ),
        name="fetch",
    )(entity_rows, asked, hub_part, relation_ids, relations)


def return_kernel(doms, works, cap, hub_ref, far_ref, want_ref, part_ref, ent_ref, state_ref,
                  rows_out, state_out,
                  back, xbuf, part_buf, r2, total, r3,
                  x_send, x_recv, far_send, far_recv, r2_send, r2_recv, r3_send, r3_recv):
    dom, work = lax.axis_index("dom"), lax.axis_index("work")
    me = dom * works + work
    core, line = lax.rem(work, 2), work // 2
    lines = works // 2
    count = doms * works
    own, width = ent_ref.shape
    part = own // doms
    msg = cap * 4
    greet(doms, works)

    def swap(y, carry):
        start = pl.multiple_of((y * 2 + 1 - core) * own, own)
        pltpu.make_async_remote_copy(
            src_ref=hub_ref.at[pl.ds(start, own), :], dst_ref=xbuf.at[y],
            send_sem=x_send, recv_sem=x_recv.at[y],
            device_id=(dom, line * 2 + 1 - core), device_id_type=MESH,
        ).start()
        return carry

    lax.fori_loop(0, lines, swap, 0)

    def far_rows(p):
        return far_ref.at[pl.ds(pl.multiple_of(p * msg, msg), msg), :]

    pltpu.make_async_copy(far_rows(me), back.at[me], far_recv).start()

    def give(i, carry):
        pd, pw = ring(dom, i // works, doms), ring(work, lax.rem(i, works), works)
        pltpu.make_async_remote_copy(
            src_ref=far_rows(pd * works + pw), dst_ref=back.at[me],
            send_sem=far_send, recv_sem=far_recv, device_id=(pd, pw), device_id_type=MESH,
        ).start()
        return carry

    lax.fori_loop(1, count, give, 0)

    def add_pair(y, carry):
        arrived(xbuf.at[y], x_recv.at[y])
        start = pl.multiple_of((y * 2 + core) * own, own)
        part_buf[y] = hub_ref[pl.ds(start, own), :] + xbuf[y]
        return carry

    lax.fori_loop(0, lines, add_pair, 0)

    def piece(y, d):
        return part_buf.at[y, pl.ds(pl.multiple_of(d * part, part), part), :]

    slot = dom * lines + line
    pltpu.make_async_copy(piece(line, dom), r2.at[slot], r2_recv).start()

    def scatter(i, carry):
        pd, py = ring(dom, i // lines, doms), ring(line, lax.rem(i, lines), lines)
        pltpu.make_async_remote_copy(
            src_ref=piece(py, pd), dst_ref=r2.at[slot],
            send_sem=r2_send, recv_sem=r2_recv, device_id=(pd, py * 2 + core), device_id_type=MESH,
        ).start()
        return carry

    lax.fori_loop(1, doms * lines, scatter, 0)
    arrived(r2, r2_recv)
    total[...] = jnp.sum(r2[...], axis=0)

    pltpu.make_async_copy(total, r3.at[dom], r3_recv).start()

    def hand(i, carry):
        pltpu.make_async_remote_copy(
            src_ref=total, dst_ref=r3.at[dom],
            send_sem=r3_send, recv_sem=r3_recv, device_id=(ring(dom, i, doms), work), device_id_type=MESH,
        ).start()
        return carry

    lax.fori_loop(1, doms, hand, 0)

    arrived(back, far_recv)
    wanted = want_ref[:, 0, :].T
    row = lax.broadcasted_iota(jnp.int32, (own, count), 0)
    flat = back.reshape(count * msg, 128)
    sums = [jnp.zeros((own, 128), F32) for _ in range(4)]
    for c in range(cap):
        hot = (row == wanted[c:c + 1, :]).astype(F32)
        for k in range(4):
            got = flat[pl.ds(c * 4 + k, count, stride=msg), :]
            sums[k] += jnp.dot(hot, got, preferred_element_type=F32, precision=lax.Precision.HIGHEST)

    arrived(r3, r3_recv)
    owner = dom == part_ref[0]
    hub_sum = r3[...].reshape(own, width)
    grads = [s + jnp.where(owner, hub_sum[:, k * 128:(k + 1) * 128], 0.0) for k, s in enumerate(sums)]
    square = sum(g * g for g in grads)
    mean = jnp.sum(square, axis=1, keepdims=True) * (1.0 / width)
    old = jnp.broadcast_to(state_ref[...], (128, own)).T
    new = old + mean
    scale = 0.1 / (jnp.sqrt(new) + 1e-10)
    for k, g in enumerate(grads):
        rows_out[:, k * 128:(k + 1) * 128] = ent_ref[:, k * 128:(k + 1) * 128] - g * scale
    state_out[...] = new.T[0:1, :]

    arrived(xbuf, x_send)
    arrived(back.at[pl.ds(0, count - 1)], far_send)
    arrived(r2.at[pl.ds(0, doms * lines - 1)], r2_send)
    arrived(r3.at[pl.ds(0, doms - 1)], r3_send)


def give_back(doms, works, hub_grad, far_grad, wanted, hub_part, entity_rows, state):
    own, width = entity_rows.shape
    count = doms * works
    cap = 4
    lines = works // 2
    part = own // doms
    vmem, smem = pl.BlockSpec(memory_space=pltpu.VMEM), pl.BlockSpec(memory_space=pltpu.SMEM)
    dma = pltpu.SemaphoreType.DMA
    return pl.pallas_call(
        functools.partial(return_kernel, doms, works, cap),
        in_specs=[vmem, vmem, vmem, smem, vmem, vmem],
        out_specs=[vmem, vmem],
        out_shape=[
            jax.ShapeDtypeStruct((own, width), F32),
            jax.ShapeDtypeStruct((1, own), F32),
        ],
        scratch_shapes=[
            pltpu.VMEM((count, cap * 4, 128), F32),
            pltpu.VMEM((lines, own, width), F32),
            pltpu.VMEM((lines, own, width), F32),
            pltpu.VMEM((doms * lines, part, width), F32),
            pltpu.VMEM((part, width), F32),
            pltpu.VMEM((doms, part, width), F32),
            dma, dma((lines,)), dma, dma, dma, dma, dma, dma,
        ],
        compiler_params=pltpu.CompilerParams(
            collective_id=1, has_side_effects=True, vmem_limit_bytes=48 * 1024 * 1024
        ),
        name="give_back",
    )(hub_grad, far_grad, wanted, hub_part, entity_rows, state)


def per_device(doms, works, entity_rows, adagrad_state, relations, hub_part, requests,
               source_slot, relation_ids, target_slot, negative_slot):
    own = entity_rows.shape[0]
    count = doms * works
    asked = requests.reshape(count, 1, -1)
    asked = jnp.pad(asked, ((0, 0), (0, 0), (0, 128 - asked.shape[2])))
    w_lin, wanted, rel_rows = fetch(
        doms, works, entity_rows, asked, hub_part, relation_ids.reshape(-1), relations
    )
    hub_grad, far_grad = train(w_lin, rel_rows, source_slot, target_slot, negative_slot, works * own)
    new_rows, new_state = give_back(
        doms, works, hub_grad, far_grad, wanted, hub_part, entity_rows, adagrad_state.reshape(1, own)
    )
    return new_rows, new_state.reshape(own)


def solution(mesh):
    doms, works = mesh.shape["dom"], mesh.shape["work"]
    both = ("dom", "work")
    return jax.shard_map(
        functools.partial(per_device, doms, works),
        mesh=mesh,
        in_specs=(
            P(both, None), P(both), P(), P(), P(both, None), P(both, None),
            P(both, None), P(both, None), P(both, None, None),
        ),
        out_specs=(P(both, None), P(both)),
        check_vma=False,
    )
```

time: 604 us -> 162 us (0.27)
  waiting for transfers between devices: 254 us -> 0 us
  Pallas kernels: 0 us -> 146 us
  other arithmetic: 127 us -> 1.34 us
  matrix products: 107 us -> 0 us
  local copies, waits for them, and re-layouts: 73.2 us -> 11.9 us
  starting transfers between devices: 23.5 us -> 0 us
  between operations: 15 us -> 1.34 us
    psum x2 -> x0, waiting for transfers between devices: 216 us -> none  [the longest x1 126 us: per_device(): hub_total = lax.psum(hub_grad, ('dom', 'work'))]
    pallas_call x0 -> x3, Pallas kernels: none -> 146 us  [the longest x1 53.1 us: train(): pl.pallas_call(functools.partial(train_kernel, tiles), grid_spec=pltpu.Pr...]
    dot_general x12 -> x0, matrix products: 107 us -> none  [the longest x6 53.4 us: bucket_loss(): jnp.einsum('ed,nd->en', query, working[negatives[1]], precision=lax.Preci...]
    scatter-add x9 -> x0, other arithmetic: 81.7 us -> none  [the longest x2 23.3 us: bucket_loss(): tail_rows = working[target]]
    gather x12 -> x0, local copies, waits for them, and re-layouts: 60.4 us -> none  [the longest x2 17.4 us: bucket_loss(): rel_rows = relations[relation]]
    all_to_all x3 -> x0, waiting for transfers between devices: 38.2 us -> none  [the longest x1 19.5 us: per_device(): lax.all_to_all(far_grad, ('dom', 'work'), split_axis=0, concat_axis=0, ti...]
    add_any x6 -> x0, other arithmetic: 25.1 us -> none  [the longest x2 9.78 us: bucket_loss(): working[negatives[1]]]
    all_to_all x3 -> x0, starting transfers between devices: 23.4 us -> none  [the longest x1 9.84 us: per_device(): lax.all_to_all(entity_rows[wanted], ('dom', 'work'), split_axis=0, concat...]
  transfers between devices with their start and end apart: 6 -> 0, of which waited for: 4 -> 0; matrix products, arithmetic and copies ran while one was open for 5% -> 0% of each run, Pallas kernels for 0% -> 0%
where the time goes in v1:
time: 162 us; the launch traced here: 161 us
  Pallas kernels  146 us (90%)
  local copies, waits for them, and re-layouts  11.9 us (7%)
    pallas_call x1, Pallas kernels, train(): pl.pallas_call(functools.partial(train_kernel, tiles), grid_spec=pltpu.Pr...  53.1 us
    pallas_call x1, Pallas kernels, fetch(): pl.pallas_call(functools.partial(fetch_kernel, doms, works, cap), in_spec...  49.5 us
    pallas_call x1, Pallas kernels, give_back(): pl.pallas_call(functools.partial(return_kernel, doms, works, cap), in_spe...  43.7 us
    unnamed x16, local copies, waits for them, and re-layouts  7.85 us

profile of v1, /device:TPU:1, one launch (start us, length us, event | category | flops | bytes accessed | tf_op | source)
XLA Modules:
  0.0 160.9 jit_solution(4703668650107273086)
XLA Ops:
  1.3 0.5 broadcast.5
  1.8 1.3 reduce.3
  3.1 0.7 copy.18
  3.8 1.3 reshape.32.src_v
  5.1 1.3 reshape.33.tgt_v
  6.5 1.3 copy_bitcast_fusion.1
  7.8 0.1 reshape.30
  7.9 0.0 copy-start.2
  8.0 0.9 copy-done.2
  8.9 49.5 %fetch.1 = (f32[6144,128]{1,0:T(8,128)S(1)}, s32[128,1,128]{2,1,0:T(1,128)S(1)}, f32[2048,512]{1,0:T(8,128)}) custom-call(f32[128,512]{1,0:T(8,128)S(1)} %copy-done.2, s32[128,1,128]{2,1,0:T(1,128)S(1)} %pad.4.req_ref, s32[1]{0:T(128)S(6)} %copy.21.hub_ref.part_ref, s32[2048]{0:T(1024)S(1)} %bitcast.13, f32[4096,512]{1,0:T(8,128)} %rel_hbm.1), custom_call_target="tpu_custom_call" | custom-call | tf_op jit(solution)/shard_map/fetch/pallas_call | solution.py:330
  58.4 0.0 copy-start
  58.4 1.7 %copy-done = f32[6144,128]{1,0:T(8,128)} copy-done((f32[6144,128]{1,0:T(8,128)}, f32[6144,128]{1,0:T(8,128)S(1)}, u32[]{:S(2)}) %copy-start) | copy-done | bytes 3145752
  60.0 0.0 copy-start.3
  60.0 0.0 copy-start.5
  60.1 53.1 %train.1 = (f32[1024,512]{1,0:T(8,128)}, f32[2048,128]{1,0:T(8,128)}) custom-call(s32[2048]{0:T(1024)} %get-tuple-element.17.src_s, s32[2048]{0:T(1024)} %get-tuple-element.16.tgt_s, f32[6144,128]{1,0:T(8,128)} %copy-done, f32[2048,512]{1,0:T(8,128)} %get-tuple-element.10.rel_ref, s32[8,1,256]{2,1,0:T(1,128)} %reshape.32.src_v, s32[8,1,256]{2,1,0:T(1,128)} %reshape.33.tgt_v, ...), custom_call_target="tpu_custom_call" | custom-call | tf_op jit(solution)/shard_map/train/pallas_call | solution.py:138
  113.2 0.0 copy-done.3
  113.2 0.0 copy-done.5
  113.2 0.0 copy-start.1
  113.2 1.6 copy-done.1
  114.8 0.0 copy-start.4
  114.8 1.2 copy-done.4
  116.0 43.7 %give_back.1 = (f32[128,512]{1,0:T(8,128)S(1)}, f32[1,128]{1,0:T(1,128)S(1)}) custom-call(f32[1024,512]{1,0:T(8,128)S(1)} %copy-done.1, f32[2048,128]{1,0:T(8,128)S(1)} %copy-done.4, s32[128,1,128]{2,1,0:T(1,128)S(1)} %get-tuple-element.13.want_ref, s32[1]{0:T(128)S(6)} %copy.21.hub_ref.part_ref, f32[128,512]{1,0:T(8,128)S(1)} %copy-done.3, ...), custom_call_target="tpu_custom_call" | custom-call | tf_op jit(solution)/shard_map/give_back/pallas_call | solution.py:471
  159.7 0.7 copy.22
  160.4 0.5 copy.23
  (1 shorter events, 0.0 us)
Async XLA Ops:
  7.9 1.0 copy-start.2
  58.4 1.7 %copy-start = (f32[6144,128]{1,0:T(8,128)}, f32[6144,128]{1,0:T(8,128)S(1)}, u32[]{:S(2)}) copy-start(f32[6144,128]{1,0:T(8,128)S(1)} %get-tuple-element.9.w_ref) | copy-start | bytes 9437188
  60.0 53.1 %copy-start.3 = (f32[128,512]{1,0:T(8,128)S(1)}, f32[128,512]{1,0:T(8,128)}, u32[]{:S(2)}) copy-start(f32[128,512]{1,0:T(8,128)} %ent_ref.3) | copy-start | bytes 786436
  60.0 53.1 %copy-start.5 = (f32[128]{0:T(128)S(1)}, f32[128]{0:T(128)}, u32[]{:S(2)}) copy-start(f32[128]{0:T(128)} %param.10) | copy-start | bytes 1540
  113.2 1.6 copy-start.1
  114.8 1.2 copy-start.4

commit v2 on v0

v2 whole, which is shorter than its diff:
```python
import functools
import jax
import jax.numpy as jnp
from jax import lax
from jax.experimental import pallas as pl
from jax.experimental.pallas import tpu as pltpu
from jax.sharding import PartitionSpec as P

F32 = jnp.float32
BF16 = jnp.bfloat16
NT = (((1,), (1,)), ((), ()))
MESH = pl.DeviceIdType.MESH
MIB = 1024 * 1024
CAP = 4
SIDE = 4


def ring(at, by, size):
    return lax.rem(at + by, size)


def for_peers(dom, work, doms, works, act, first=0, last=None):
    near = [ring(work, k, works) for k in range(works)]
    if first == 0:
        for pw in near[1:]:
            act(dom, pw)

    def along(i, carry):
        pd = ring(dom, i, doms)
        for pw in near:
            act(pd, pw)
        return carry

    lax.fori_loop(max(first, 1), last or doms, along, 0)


def greet(doms, works):
    dom, work = lax.axis_index("dom"), lax.axis_index("work")
    barrier = pltpu.get_barrier_semaphore()

    def call(pd, pw):
        pl.semaphore_signal(barrier, inc=1, device_id=(pd, pw), device_id_type=MESH)

    for_peers(dom, work, doms, works, call)


def greeted(doms, works):
    pl.semaphore_wait(pltpu.get_barrier_semaphore(), doms * works - 1)


def arrived(ref, sem):
    pltpu.make_async_copy(ref, ref, sem).wait()


def send(src, dst, sent, landed, device):
    pltpu.make_async_remote_copy(
        src_ref=src, dst_ref=dst, send_sem=sent, recv_sem=landed, device_id=device, device_id_type=MESH
    ).start()


def cols(c):
    return slice(c * 128, (c + 1) * 128)


def fetch_kernel(doms, works, ent_ref, req_ref, hub_ref, ids_ref, rel_hbm,
                 w_ref, want_ref, rel_ref,
                 erow, hub1, piece, out_buf, reqv, want_s, relv,
                 rel_sem, req_send, req_recv, loc_sem, h1_send, h1_recv, h2_send, h2_recv,
                 x_send, x_recv, far_send, far_recv):
    dom, work = lax.axis_index("dom"), lax.axis_index("work")
    me = dom * works + work
    core, line = lax.rem(work, 2), work // 2
    z, x = dom // SIDE, lax.rem(dom, SIDE)
    lines = works // 2
    count = doms * works
    own = ent_ref.shape[0]
    half = own // 2
    part = half // doms
    hub = works * own
    per_row = 128 // CAP

    load = pltpu.make_async_copy(rel_hbm, relv, rel_sem)
    load.start()
    greet(doms, works)
    for c in range(4):
        erow[:, c, :] = ent_ref[:, cols(c)]
    for j in range(count // per_row):
        reqv[j] = req_ref[:, cols(j)]
    greeted(doms, works)

    for s in range(2):
        hub1[s, dom] = erow[pl.ds(s * half + dom * part, part)]

    def spread(i, carry):
        pd = ring(dom, i, doms)
        for s in range(2):
            send(erow.at[pl.ds(s * half + pd * part, part)], hub1.at[s, dom], h1_send, h1_recv, (pd, work))
        return carry

    lax.fori_loop(1, doms, spread, 0)

    want_ref[me] = reqv[me // per_row]

    def ask(pd, pw):
        send(reqv.at[(pd * works + pw) // per_row], want_ref.at[me], req_send, req_recv, (pd, pw))

    for_peers(dom, work, doms, works, ask)
    arrived(hub1.at[:, pl.ds(0, doms - 1)], h1_recv)

    def rows(s, y, d, n):
        return w_ref.at[pl.ds((y * 2 + core) * own + s * half + d * part, n * part)]

    at = hub_ref[0]
    for s in range(2):
        piece[s] = hub1[s, at]
    for s in range(2):
        copy = pltpu.make_async_copy(piece.at[s], rows(s, line, dom, 1), loc_sem)
        copy.start()
        copy.wait()

    def along_x(k):
        return (z * SIDE + ring(x, k, SIDE), work)

    def along_z(k):
        return (ring(z, k, SIDE) * SIDE + x, work)

    def along_y(k):
        return (dom, ring(line, k, lines) * 2 + core)

    around = (1, SIDE - 1, 2)

    def hop(refs, s, step, to):
        for k in around:
            for ref in refs:
                send(ref, ref, h2_send, h2_recv.at[s, step], to(k))

    def landed(s, step, n):
        arrived(w_ref.at[pl.ds(0, (SIDE - 1) * n * part)], h2_recv.at[s, step])

    hop([rows(0, line, dom, 1)], 0, 0, along_x)
    hop([rows(1, line, dom, 1)], 1, 0, along_y)

    arrived(want_ref.at[pl.ds(0, count - 1)], req_recv)
    copy = pltpu.make_async_copy(want_ref, want_s, loc_sem)
    copy.start()
    copy.wait()
    lane = lax.rem(me, per_row) * CAP

    def fill(p):
        for c in range(CAP):
            out_buf[p, c] = erow[want_s[p, 0, lane + c]]

    def far_rows(p):
        return w_ref.at[pl.ds(hub + p * CAP, CAP)]

    fill(me)
    pltpu.make_async_copy(out_buf.at[me], far_rows(me), far_recv).start()

    def answer(pd, pw):
        p = pd * works + pw
        fill(p)
        send(out_buf.at[p], far_rows(me), far_send, far_recv, (pd, pw))

    cuts = [0, 1, doms // 4, doms]
    for_peers(dom, work, doms, works, answer, cuts[0], cuts[1])
    landed(0, 0, 1)
    hop([rows(0, line, z * SIDE, SIDE)], 0, 1, along_z)
    landed(1, 0, 1)
    hop([rows(1, y, dom, 1) for y in range(lines)], 1, 1, along_x)
    for_peers(dom, work, doms, works, answer, cuts[1], cuts[2])
    landed(0, 1, SIDE)
    hop([rows(0, line, 0, doms)], 0, 2, along_y)
    landed(1, 1, lines)
    hop([rows(1, y, z * SIDE, SIDE) for y in range(lines)], 1, 2, along_z)
    for_peers(dom, work, doms, works, answer, cuts[2], cuts[3])

    landed(0, 2, doms)
    landed(1, 2, lines * SIDE)
    for y in range(lines):
        mine = w_ref.at[pl.ds((y * 2 + core) * own, own)]
        send(mine, mine, x_send, x_recv, (dom, line * 2 + 1 - core))
    load.wait()

    buckets, edges = ids_ref.shape
    for b in range(buckets):
        def pick(e, carry, b=b):
            rel_ref[b * edges + e] = relv[ids_ref[b, e]]
            return carry

        lax.fori_loop(0, edges, pick, 0, unroll=8)

    swapped = w_ref.at[pl.ds(0, hub // 2)]
    arrived(swapped, x_recv)
    arrived(w_ref.at[pl.ds(hub, count * CAP)], far_recv)
    arrived(swapped, x_send)
    arrived(w_ref.at[pl.ds(0, 2 * (doms * lines - 1) * part)], h2_send)
    arrived(hub1.at[:, pl.ds(0, doms - 1)], h1_send)
    arrived(out_buf.at[pl.ds(0, count - 1)], far_send)
    arrived(want_ref.at[pl.ds(0, count - 1)], req_send)


def fetch(doms, works, entity_rows, requests, hub_part, relation_ids, relations):
    own, width = entity_rows.shape
    count = doms * works
    part = own // 2 // doms
    vmem, smem = pl.BlockSpec(memory_space=pltpu.VMEM), pl.BlockSpec(memory_space=pltpu.SMEM)
    dma = pltpu.SemaphoreType.DMA
    return pl.pallas_call(
        functools.partial(fetch_kernel, doms, works),
        in_specs=[vmem, vmem, smem, smem, pl.BlockSpec(memory_space=pl.ANY)],
        out_specs=[vmem, vmem, vmem],
        out_shape=[
            jax.ShapeDtypeStruct((works * own + count * CAP, 4, 128), F32),
            jax.ShapeDtypeStruct((count, 1, 128), jnp.int32),
            jax.ShapeDtypeStruct((relation_ids.size, width), F32),
        ],
        scratch_shapes=[
            pltpu.VMEM((own, 4, 128), F32),
            pltpu.VMEM((2, doms, part, 4, 128), F32),
            pltpu.VMEM((2, part, 4, 128), F32),
            pltpu.VMEM((count, CAP, 4, 128), F32),
            pltpu.VMEM((count * CAP // 128, 1, 128), jnp.int32),
            pltpu.SMEM((count, 1, 128), jnp.int32),
            pltpu.VMEM(relations.shape, F32),
            dma, dma, dma, dma, dma, dma, dma, dma((2, 3)), dma, dma, dma, dma,
        ],
        compiler_params=pltpu.CompilerParams(
            collective_id=0, has_side_effects=True, vmem_limit_bytes=48 * MIB
        ),
        name="fetch",
    )(entity_rows, requests, hub_part, relation_ids, relations)


def train_kernel(doms, works, src_s, tgt_s, part_ref, w_ref, rel_ref, src_v, tgt_v, neg_ref, want_ref,
                 ent_ref, state_ref, rows_out, state_out,
                 wb, wbt, cnt, slot_v, gt, rneg, rhi, rlo, hlin, tlin, qf, slope_v, dneg,
                 acc, far_lin, theirs, mine, back, xbuf, r2, total, r3, want_t,
                 x_send, x_recv, far_send, far_recv, r2_send, r2_recv, r3_send, r3_recv):
    dom, work = lax.axis_index("dom"), lax.axis_index("work")
    me = dom * works + work
    core, line = lax.rem(work, 2), work // 2
    lines = works // 2
    count = doms * works
    own, width = ent_ref.shape
    hub = works * own
    slots = wb.shape[0]
    buckets, _, negs = neg_ref.shape
    edges = slot_v.shape[2]
    tiles = src_v.shape[1] // edges
    steps = buckets * tiles
    part = own // doms
    msg = CAP * 4
    greet(doms, works)

    for c in range(4):
        column = w_ref[:, c, :]
        wb[:, cols(c)] = column.astype(BF16)
        wbt[cols(c), :] = column.T.astype(BF16)
    for i in range(steps):
        spot = slice(i % tiles * edges, (i % tiles + 1) * edges)
        slot_v[2 * i] = src_v[i // tiles:i // tiles + 1, spot]
        slot_v[2 * i + 1] = tgt_v[i // tiles:i // tiles + 1, spot]

    high = lax.broadcasted_iota(jnp.int32, (16, negs), 0)
    low = lax.broadcasted_iota(jnp.int32, (128, negs), 0)
    for b in range(buckets):
        for side in range(2):
            slot = neg_ref[b, side:side + 1, :]
            top = (high == lax.shift_right_logical(slot, 7)).astype(F32).astype(BF16)
            end = (low == jnp.bitwise_and(slot, 127)).astype(F32).astype(BF16)
            table = lax.dot_general(end, top, NT, preferred_element_type=F32) * (0.5 / negs)
            for g in range(slots // 128):
                cnt[b * 2 + side, cols(g), :] = jnp.broadcast_to(table[:, g:g + 1], (128, 128))

    block = 128

    def step(i, carry):
        b, first = i // tiles, lax.rem(i, tiles) * edges
        base = i * edges

        def gather(e, carry):
            at = pl.ds(pl.multiple_of(e * 4, 4), 4)
            hlin[at, :] = w_ref[src_s[b, first + e]]
            tlin[at, :] = w_ref[tgt_s[b, first + e]]
            return carry

        lax.fori_loop(0, edges, gather, 0, unroll=8)

        def forward(k, carry):
            row = pl.multiple_of(k * block, block)
            here = pl.ds(row, block)
            there = pl.ds(pl.multiple_of(base + row, block), block)
            query = pl.ds(pl.multiple_of(2 * base + row, block), block)
            mirror = pl.ds(pl.multiple_of(2 * base + edges + row, block), block)
            score = jnp.zeros((block, 128), F32)
            for p in range(2):
                q = p + 2
                hr, hi = (hlin[pl.ds(4 * row + c, block, stride=4), :] for c in (p, q))
                tr, ti = (tlin[pl.ds(4 * row + c, block, stride=4), :] for c in (p, q))
                rr, ri = rel_ref[there, cols(p)], rel_ref[there, cols(q)]
                qr = hr * rr - hi * ri
                qi = hr * ri + hi * rr
                score = score + (qr * tr + qi * ti)
                qf[here, cols(p)] = qr
                qf[here, cols(q)] = qi
                rneg[query, cols(p)] = qr.astype(BF16)
                rneg[query, cols(q)] = qi.astype(BF16)
                rneg[mirror, cols(p)] = (rr * tr + ri * ti).astype(BF16)
                rneg[mirror, cols(q)] = (rr * ti - ri * tr).astype(BF16)
            positive = jnp.sum(score, axis=1, keepdims=True)
            slope_v[here, :] = jnp.broadcast_to(0.5 * jnp.tanh(0.5 * positive) - 0.5, (block, 128))
            return carry

        lax.fori_loop(0, edges // block, forward, 0)

        for side in range(2):
            there = pl.ds(pl.multiple_of(2 * base + side * edges, edges), edges)
            for m in range(slots // 512):
                rows = slice(m * 512, (m + 1) * 512)
                st = lax.dot_general(wb[rows, :], rneg[there, :], NT, preferred_element_type=F32)
                weight = cnt[b * 2 + 1 - side, rows, :]
                weight = jnp.concatenate([weight] * (edges // 128), axis=1)
                gt[rows, there] = (weight * jnp.tanh(0.5 * st) + weight).astype(BF16)
            dneg[side] = jnp.dot(wbt[...], gt[:, there], preferred_element_type=F32)

        def backward(k, carry):
            row = pl.multiple_of(k * block, block)
            here = pl.ds(row, block)
            there = pl.ds(pl.multiple_of(base + row, block), block)
            source = pl.ds(pl.multiple_of(2 * base + row, block), block)
            target = pl.ds(pl.multiple_of(2 * base + edges + row, block), block)

            def put(at, c, value):
                top = value.astype(BF16)
                rhi[at, cols(c)] = top
                rlo[at, cols(c)] = (value - top.astype(F32)).astype(BF16)

            slope = slope_v[here, :]
            for p in range(2):
                q = p + 2
                rr, ri = rel_ref[there, cols(p)], rel_ref[there, cols(q)]
                tr, ti = (tlin[pl.ds(4 * row + c, block, stride=4), :] for c in (p, q))
                dqr = slope * tr + dneg[0, cols(p), here].T
                dqi = slope * ti + dneg[0, cols(q), here].T
                put(source, p, dqr * rr + dqi * ri)
                put(source, q, dqi * rr - dqr * ri)
                dur = dneg[1, cols(p), here].T
                dui = dneg[1, cols(q), here].T
                put(target, p, slope * qf[here, cols(p)] + (dur * rr - dui * ri))
                put(target, q, slope * qf[here, cols(q)] + (dur * ri + dui * rr))
            return carry

        lax.fori_loop(0, edges // block, backward, 0)
        return carry

    lax.fori_loop(0, steps, step, 0)

    def gradient(starts, beside):
        acc[...] = jnp.zeros_like(acc)

        def chunk(k, carry):
            at = pl.ds(pl.multiple_of(k * edges, edges), edges)
            slot = slot_v[k]
            number = lax.broadcasted_iota(jnp.int32, (own, edges), 0)
            hot = jnp.concatenate(
                [(number == slot - start).astype(F32).astype(BF16) for start in starts], axis=0
            )
            weight = jnp.concatenate([gt[pl.ds(start, own), at] for start in starts], axis=0)
            acc[...] += (
                jnp.dot(weight, rneg[at, :], preferred_element_type=F32)
                + jnp.dot(hot, rhi[at, :], preferred_element_type=F32)
                + jnp.dot(hot, rlo[at, :], preferred_element_type=F32)
            )
            beside(k)
            return carry

        lax.fori_loop(0, 2 * steps, chunk, 0)

    gradient([hub + j * own for j in range(count * CAP // own)], lambda k: None)
    for c in range(4):
        far_lin[pl.ds(c, count * CAP, stride=4), :] = acc[:, cols(c)]
    greeted(doms, works)

    def far_rows(p):
        return far_lin.at[pl.ds(pl.multiple_of(p * msg, msg), msg), :]

    pltpu.make_async_copy(far_rows(me), back.at[me], far_recv).start()
    share = count // (4 * steps)

    def give(from_step):
        def some(k):
            for n in range(share):
                i = (from_step + k) * share + n

                @pl.when(i > 0)
                def _():
                    pd, pw = ring(dom, i // works, doms), ring(work, lax.rem(i, works), works)
                    send(far_rows(pd * works + pw), back.at[me], far_send, far_recv, (pd, pw))

        return some

    def starts(of):
        return [pl.multiple_of((y * 2 + of) * own, own) for y in range(lines)]

    gradient(starts(1 - core), give(0))
    theirs[...] = acc[...].reshape(lines, own, width)
    for y in range(lines):
        send(theirs.at[y], xbuf.at[y], x_send, x_recv.at[y], (dom, line * 2 + 1 - core))
    gradient(starts(core), give(2 * steps))

    for y in range(lines):
        arrived(xbuf.at[y], x_recv.at[y])
        mine[y] = acc[y * own:(y + 1) * own, :] + xbuf[y]

    def piece(y, d):
        return mine.at[y, pl.ds(pl.multiple_of(d * part, part), part), :]

    slot = dom * lines + line
    pltpu.make_async_copy(piece(line, dom), r2.at[slot], r2_recv).start()

    def scatter(i, carry):
        pd, py = ring(dom, i // lines, doms), ring(line, lax.rem(i, lines), lines)
        send(piece(py, pd), r2.at[slot], r2_send, r2_recv, (pd, py * 2 + core))
        return carry

    lax.fori_loop(1, doms * lines, scatter, 0)

    want_t[...] = want_ref[:, 0, :].T
    arrived(back, far_recv)
    lane = lax.rem(me, 128 // CAP) * CAP
    row = lax.broadcasted_iota(jnp.int32, (own, count), 0)
    flat = back.reshape(count * msg, 128)
    sums = [jnp.zeros((own, 128), F32) for _ in range(4)]
    for c in range(CAP):
        hot = (row == want_t[pl.ds(lane + c, 1), :]).astype(F32)
        for k in range(4):
            got = flat[pl.ds(c * 4 + k, count, stride=msg), :]
            sums[k] += jnp.dot(hot, got, preferred_element_type=F32, precision=lax.Precision.HIGHEST)
    for k in range(4):
        acc[0:own, cols(k)] = sums[k]

    arrived(r2, r2_recv)
    total[...] = jnp.sum(r2[...], axis=0)
    pltpu.make_async_copy(total, r3.at[dom], r3_recv).start()

    def hand(i, carry):
        send(total, r3.at[dom], r3_send, r3_recv, (ring(dom, i, doms), work))
        return carry

    lax.fori_loop(1, doms, hand, 0)
    arrived(r3, r3_recv)
    owner = dom == part_ref[0]
    hub_sum = r3[...].reshape(own, width)
    grads = [acc[0:own, cols(k)] + jnp.where(owner, hub_sum[:, cols(k)], 0.0) for k in range(4)]
    square = sum(g * g for g in grads)
    mean = jnp.sum(square, axis=1, keepdims=True) * (1.0 / width)
    old = jnp.broadcast_to(state_ref[...], (128, own)).T
    new = old + mean
    scale = 0.1 / (jnp.sqrt(new) + 1e-10)
    for k, g in enumerate(grads):
        rows_out[:, cols(k)] = ent_ref[:, cols(k)] - g * scale
    state_out[...] = new.T[0:1, :]

    arrived(xbuf, x_send)
    arrived(back.at[pl.ds(0, count - 1)], far_send)
    arrived(r2.at[pl.ds(0, doms * lines - 1)], r2_send)
    arrived(r3.at[pl.ds(0, doms - 1)], r3_send)


def train(doms, works, w_rows, rel_rows, source, target, negative, wanted, hub_part, entity_rows, state,
          edges=512):
    own, width = entity_rows.shape
    count = doms * works
    lines = works // 2
    part = own // doms
    slots = w_rows.shape[0]
    total = source.size
    vmem, smem = pl.BlockSpec(memory_space=pltpu.VMEM), pl.BlockSpec(memory_space=pltpu.SMEM)
    dma = pltpu.SemaphoreType.DMA
    return pl.pallas_call(
        functools.partial(train_kernel, doms, works),
        in_specs=[smem] * 3 + [vmem] * 8,
        out_specs=[vmem, vmem],
        out_shape=[
            jax.ShapeDtypeStruct((own, width), F32),
            jax.ShapeDtypeStruct((1, own), F32),
        ],
        scratch_shapes=[
            pltpu.VMEM((slots, width), BF16),
            pltpu.VMEM((width, slots), BF16),
            pltpu.VMEM((2 * source.shape[0], slots, 128), F32),
            pltpu.VMEM((2 * total // edges, 1, edges), jnp.int32),
            pltpu.VMEM((slots, 2 * total), BF16),
            pltpu.VMEM((2 * total, width), BF16),
            pltpu.VMEM((2 * total, width), BF16),
            pltpu.VMEM((2 * total, width), BF16),
            pltpu.VMEM((edges * 4, 128), F32),
            pltpu.VMEM((edges * 4, 128), F32),
            pltpu.VMEM((edges, width), F32),
            pltpu.VMEM((edges, 128), F32),
            pltpu.VMEM((2, width, edges), F32),
            pltpu.VMEM((lines * own, width), F32),
            pltpu.VMEM((count * CAP * 4, 128), F32),
            pltpu.VMEM((lines, own, width), F32),
            pltpu.VMEM((lines, own, width), F32),
            pltpu.VMEM((count, CAP * 4, 128), F32),
            pltpu.VMEM((lines, own, width), F32),
            pltpu.VMEM((doms * lines, part, width), F32),
            pltpu.VMEM((part, width), F32),
            pltpu.VMEM((doms, part, width), F32),
            pltpu.VMEM((128, count), jnp.int32),
            dma, dma((lines,)), dma, dma, dma, dma, dma, dma,
        ],
        compiler_params=pltpu.CompilerParams(
            collective_id=1, has_side_effects=True, vmem_limit_bytes=60 * MIB
        ),
        name="train",
    )(source, target, hub_part, w_rows, rel_rows, source, target, negative, wanted, entity_rows, state)


def per_device(doms, works, entity_rows, adagrad_state, relations, hub_part, requests,
               source_slot, relation_ids, target_slot, negative_slot):
    own = entity_rows.shape[0]
    w_rows, wanted, rel_rows = fetch(
        doms, works, entity_rows, requests, hub_part, relation_ids, relations
    )
    new_rows, new_state = train(
        doms, works, w_rows, rel_rows, source_slot, target_slot, negative_slot, wanted, hub_part,
        entity_rows, adagrad_state.reshape(1, own)
    )
    return new_rows, new_state.reshape(own)


def solution(mesh):
    doms, works = mesh.shape["dom"], mesh.shape["work"]
    both = ("dom", "work")
    return jax.shard_map(
        functools.partial(per_device, doms, works),
        mesh=mesh,
        in_specs=(
            P(both, None), P(both), P(), P(), P(both, None), P(both, None),
            P(both, None), P(both, None), P(both, None, None),
        ),
        out_specs=(P(both, None), P(both)),
        check_vma=False,
    )
```

time: 604 us -> 153 us (0.25)
  waiting for transfers between devices: 254 us -> 0 us
  Pallas kernels: 0 us -> 144 us
  other arithmetic: 127 us -> 0 us
  matrix products: 107 us -> 0 us
  local copies, waits for them, and re-layouts: 73.2 us -> 7.47 us
  starting transfers between devices: 23.5 us -> 0 us
  between operations: 15 us -> 1.31 us
    psum x2 -> x0, waiting for transfers between devices: 216 us -> none  [the longest x1 126 us: per_device(): hub_total = lax.psum(hub_grad, ('dom', 'work'))]
    pallas_call x0 -> x2, Pallas kernels: none -> 144 us  [the longest x1 91.3 us: train(): pl.pallas_call(functools.partial(train_kernel, doms, works), in_specs=[sm...]
    dot_general x12 -> x0, matrix products: 107 us -> none  [the longest x6 53.4 us: bucket_loss(): jnp.einsum('ed,nd->en', query, working[negatives[1]], precision=lax.Preci...]
    scatter-add x9 -> x0, other arithmetic: 81.7 us -> none  [the longest x2 23.3 us: bucket_loss(): tail_rows = working[target]]
    gather x12 -> x0, local copies, waits for them, and re-layouts: 60.4 us -> none  [the longest x2 17.4 us: bucket_loss(): rel_rows = relations[relation]]
    all_to_all x3 -> x0, waiting for transfers between devices: 38.2 us -> none  [the longest x1 19.5 us: per_device(): lax.all_to_all(far_grad, ('dom', 'work'), split_axis=0, concat_axis=0, ti...]
    add_any x6 -> x0, other arithmetic: 25.1 us -> none  [the longest x2 9.78 us: bucket_loss(): working[negatives[1]]]
    all_to_all x3 -> x0, starting transfers between devices: 23.4 us -> none  [the longest x1 9.84 us: per_device(): lax.all_to_all(entity_rows[wanted], ('dom', 'work'), split_axis=0, concat...]
  transfers between devices with their start and end apart: 6 -> 0, of which waited for: 4 -> 0; matrix products, arithmetic and copies ran while one was open for 5% -> 0% of each run, Pallas kernels for 0% -> 0%
where the time goes in v2:
time: 153 us; the launch traced here: 152 us
  Pallas kernels  144 us (94%)
  local copies, waits for them, and re-layouts  7.47 us (5%)
    pallas_call x1, Pallas kernels, train(): pl.pallas_call(functools.partial(train_kernel, doms, works), in_specs=[sm...  91.3 us
    pallas_call x1, Pallas kernels, fetch(): pl.pallas_call(functools.partial(fetch_kernel, doms, works), in_specs=[vm...  52.2 us
    unnamed x12, local copies, waits for them, and re-layouts  7.47 us

profile of v2, /device:TPU:1, one launch (start us, length us, event | category | flops | bytes accessed | tf_op | source)
XLA Modules:
  0.0 152.3 jit_solution(6382769583848450272)
XLA Ops:
  1.3 0.0 copy-start.1
  1.3 0.9 copy-done.1
  2.2 0.0 copy-start.3
  2.2 0.7 copy-done.3
  2.9 0.0 copy-start.4
  2.9 0.7 copy-done.4
  3.6 52.2 %fetch.1 = (f32[1536,4,128]{2,1,0:T(4,128)S(1)}, s32[128,1,128]{2,1,0:T(1,128)S(1)}, f32[2048,512]{1,0:T(8,128)}) custom-call(f32[128,512]{1,0:T(8,128)S(1)} %copy-done.1, s32[1,512]{1,0:T(1,128)S(1)} %copy-done.4, s32[1]{0:T(128)S(6)} %copy.13.hub_ref.part_ref, s32[2,1024]{1,0:T(2,128)S(1)} %copy-done.3, f32[4096,512]{1,0:T(8,128)} %rel_hbm.1), custom_call_target="tpu_custom_call" | custom-call | tf_op jit(solution)/shard_map/fetch/pallas_call | solution.py:208
  55.8 0.0 copy-start
  55.8 1.7 %copy-done = f32[1536,4,128]{2,1,0:T(4,128)} copy-done((f32[1536,4,128]{2,1,0:T(4,128)}, f32[1536,4,128]{2,1,0:T(4,128)S(1)}, u32[]{:S(2)}) %copy-start) | copy-done | bytes 3145752
  57.5 0.0 copy-start.2
  57.5 0.6 copy-done.2
  58.1 91.3 %train.1 = (f32[128,512]{1,0:T(8,128)}, f32[1,128]{1,0:T(1,128)}) custom-call(s32[2,1024]{1,0:T(2,128)} %src_v.1, s32[2,1024]{1,0:T(2,128)} %tgt_v.1, s32[1]{0:T(128)S(6)} %copy.13.hub_ref.part_ref, f32[1536,4,128]{2,1,0:T(4,128)} %copy-done, f32[2048,512]{1,0:T(8,128)} %get-tuple-element.8.rel_ref, s32[2,1024]{1,0:T(2,128)} %src_v.1, s32[2,1024]{1,0:T(2,128)} %tgt_v.1, ...), custom_call_target="tpu_custom_call" | custom-call | tf_op jit(solution)/shard_map/train/pallas_call | solution.py:480
  149.5 1.7 %copy.14 = f32[128,512]{1,0:T(8,128)} copy(f32[128,512]{1,0:T(8,128)} %get-tuple-element.14) | data formatting | bytes 524288
  151.1 1.2 copy.15
Async XLA Ops:
  1.3 1.0 copy-start.1
  2.2 0.7 copy-start.3
  2.9 0.7 copy-start.4
  55.8 1.7 %copy-start = (f32[1536,4,128]{2,1,0:T(4,128)}, f32[1536,4,128]{2,1,0:T(4,128)S(1)}, u32[]{:S(2)}) copy-start(f32[1536,4,128]{2,1,0:T(4,128)S(1)} %get-tuple-element.7.w_ref) | copy-start | bytes 9437188
  57.5 0.6 copy-start.2

commit v3 on v2

--- a/solution.py
+++ b/solution.py
@@ -62,11 +62,16 @@
     return slice(c * 128, (c + 1) * 128)
 
 
-def fetch_kernel(doms, works, ent_ref, req_ref, hub_ref, ids_ref, rel_hbm,
-                 w_ref, want_ref, rel_ref,
-                 erow, hub1, piece, out_buf, reqv, want_s, relv,
-                 rel_sem, req_send, req_recv, loc_sem, h1_send, h1_recv, h2_send, h2_recv,
-                 x_send, x_recv, far_send, far_recv):
+def window_kernel(doms, works, edges, hub_ref, ids_ref, source_s, target_s, ent_hbm, req_hbm, rel_hbm,
+                  src_hbm, tgt_hbm, neg_hbm, state_hbm,
+                  rows_out, state_out,
+                  ent_ref, req_ref, src_v, tgt_v, neg_ref, state_ref,
+                  w_ref, want_ref, rel_ref, erow, hub1, piece, out_buf, reqv, want_s, relv,
+                  wb, wbt, cnt, slot_v, gt, rneg, rhi, rlo, hlin, tlin, slope_v, dneg,
+                  far_lin, back, xbuf, r2, total, r3, want_t,
+                  in_sem, rel_sem, req_send, req_recv, loc_sem, h1_send, h1_recv, h2_send, h2_recv,
+                  x_send, x_recv, far_send, far_recv,
+                  y_send, y_recv, back_send, back_recv, r2_send, r2_recv, r3_send, r3_recv):
     dom, work = lax.axis_index("dom"), lax.axis_index("work")
     me = dom * works + work
     core, line = lax.rem(work, 2), work // 2
@@ -78,10 +83,26 @@
     part = half // doms
     hub = works * own
     per_row = 128 // CAP
+    buckets, per_bucket = ids_ref.shape
+    width = ent_ref.shape[1]
+    slots = wb.shape[0]
+    negs = neg_ref.shape[2]
+    tiles = per_bucket // edges
+    steps = buckets * tiles
 
     load = pltpu.make_async_copy(rel_hbm, relv, rel_sem)
+    moves = [
+        pltpu.make_async_copy(src, dst, in_sem.at[i]) for i, (src, dst) in enumerate((
+            (ent_hbm, ent_ref), (req_hbm, req_ref), (src_hbm, src_v), (tgt_hbm, tgt_v), (neg_hbm, neg_ref),
+            (state_hbm, state_ref),
+        ))
+    ]
+    for move in moves:
+        move.start()
     load.start()
     greet(doms, works)
+    for move in moves:
+        move.wait()
     for c in range(4):
         erow[:, c, :] = ent_ref[:, cols(c)]
     for j in range(count // per_row):
@@ -174,88 +195,25 @@
     hop([rows(1, y, z * SIDE, SIDE) for y in range(lines)], 1, 2, along_z)
     for_peers(dom, work, doms, works, answer, cuts[2], cuts[3])
 
+    load.wait()
+
+    def pick(b):
+        def one(e, carry):
+            rel_ref[b * per_bucket + e] = relv[ids_ref[b, e]]
+            return carry
+
+        lax.fori_loop(0, per_bucket, one, 0, unroll=8)
+
+    for b in range(buckets - 1):
+        pick(b)
+
     landed(0, 2, doms)
     landed(1, 2, lines * SIDE)
     for y in range(lines):
         mine = w_ref.at[pl.ds((y * 2 + core) * own, own)]
         send(mine, mine, x_send, x_recv, (dom, line * 2 + 1 - core))
-    load.wait()
-
-    buckets, edges = ids_ref.shape
-    for b in range(buckets):
-        def pick(e, carry, b=b):
-            rel_ref[b * edges + e] = relv[ids_ref[b, e]]
-            return carry
-
-        lax.fori_loop(0, edges, pick, 0, unroll=8)
-
-    swapped = w_ref.at[pl.ds(0, hub // 2)]
-    arrived(swapped, x_recv)
-    arrived(w_ref.at[pl.ds(hub, count * CAP)], far_recv)
-    arrived(swapped, x_send)
-    arrived(w_ref.at[pl.ds(0, 2 * (doms * lines - 1) * part)], h2_send)
-    arrived(hub1.at[:, pl.ds(0, doms - 1)], h1_send)
-    arrived(out_buf.at[pl.ds(0, count - 1)], far_send)
-    arrived(want_ref.at[pl.ds(0, count - 1)], req_send)
-
-
-def fetch(doms, works, entity_rows, requests, hub_part, relation_ids, relations):
-    own, width = entity_rows.shape
-    count = doms * works
-    part = own // 2 // doms
-    vmem, smem = pl.BlockSpec(memory_space=pltpu.VMEM), pl.BlockSpec(memory_space=pltpu.SMEM)
-    dma = pltpu.SemaphoreType.DMA
-    return pl.pallas_call(
-        functools.partial(fetch_kernel, doms, works),
-        in_specs=[vmem, vmem, smem, smem, pl.BlockSpec(memory_space=pl.ANY)],
-        out_specs=[vmem, vmem, vmem],
-        out_shape=[
-            jax.ShapeDtypeStruct((works * own + count * CAP, 4, 128), F32),
-            jax.ShapeDtypeStruct((count, 1, 128), jnp.int32),
-            jax.ShapeDtypeStruct((relation_ids.size, width), F32),
-        ],
-        scratch_shapes=[
-            pltpu.VMEM((own, 4, 128), F32),
-            pltpu.VMEM((2, doms, part, 4, 128), F32),
-            pltpu.VMEM((2, part, 4, 128), F32),
-            pltpu.VMEM((count, CAP, 4, 128), F32),
-            pltpu.VMEM((count * CAP // 128, 1, 128), jnp.int32),
-            pltpu.SMEM((count, 1, 128), jnp.int32),
-            pltpu.VMEM(relations.shape, F32),
-            dma, dma, dma, dma, dma, dma, dma, dma((2, 3)), dma, dma, dma, dma,
-        ],
-        compiler_params=pltpu.CompilerParams(
-            collective_id=0, has_side_effects=True, vmem_limit_bytes=48 * MIB
-        ),
-        name="fetch",
-    )(entity_rows, requests, hub_part, relation_ids, relations)
-
-
-def train_kernel(doms, works, src_s, tgt_s, part_ref, w_ref, rel_ref, src_v, tgt_v, neg_ref, want_ref,
-                 ent_ref, state_ref, rows_out, state_out,
-                 wb, wbt, cnt, slot_v, gt, rneg, rhi, rlo, hlin, tlin, qf, slope_v, dneg,
-                 acc, far_lin, theirs, mine, back, xbuf, r2, total, r3, want_t,
-                 x_send, x_recv, far_send, far_recv, r2_send, r2_recv, r3_send, r3_recv):
-    dom, work = lax.axis_index("dom"), lax.axis_index("work")
-    me = dom * works + work
-    core, line = lax.rem(work, 2), work // 2
-    lines = works // 2
-    count = doms * works
-    own, width = ent_ref.shape
-    hub = works * own
-    slots = wb.shape[0]
-    buckets, _, negs = neg_ref.shape
-    edges = slot_v.shape[2]
-    tiles = src_v.shape[1] // edges
-    steps = buckets * tiles
-    part = own // doms
-    msg = CAP * 4
-    greet(doms, works)
-
-    for c in range(4):
-        column = w_ref[:, c, :]
-        wb[:, cols(c)] = column.astype(BF16)
-        wbt[cols(c), :] = column.T.astype(BF16)
+    pick(buckets - 1)
+
     for i in range(steps):
         spot = slice(i % tiles * edges, (i % tiles + 1) * edges)
         slot_v[2 * i] = src_v[i // tiles:i // tiles + 1, spot]
@@ -272,7 +230,18 @@
             for g in range(slots // 128):
                 cnt[b * 2 + side, cols(g), :] = jnp.broadcast_to(table[:, g:g + 1], (128, 128))
 
+    swapped = w_ref.at[pl.ds(0, hub // 2)]
+    arrived(swapped, x_recv)
+    arrived(w_ref.at[pl.ds(hub, count * CAP)], far_recv)
+    for c in range(4):
+        column = w_ref[:, c, :]
+        wb[:, cols(c)] = column.astype(BF16)
+        wbt[cols(c), :] = column.T.astype(BF16)
+
     block = 128
+    eighth = own // doms
+    msg = CAP * 4
+    acc, theirs, mine, qf = (relv.at[pl.ds(k * lines * own, lines * own), :] for k in range(4))
 
     def step(i, carry):
         b, first = i // tiles, lax.rem(i, tiles) * edges
@@ -280,8 +249,8 @@
 
         def gather(e, carry):
             at = pl.ds(pl.multiple_of(e * 4, 4), 4)
-            hlin[at, :] = w_ref[src_s[b, first + e]]
-            tlin[at, :] = w_ref[tgt_s[b, first + e]]
+            hlin[at, :] = w_ref[source_s[b, first + e]]
+            tlin[at, :] = w_ref[target_s[b, first + e]]
             return carry
 
         lax.fori_loop(0, edges, gather, 0, unroll=8)
@@ -356,7 +325,7 @@
     lax.fori_loop(0, steps, step, 0)
 
     def gradient(starts, beside):
-        acc[...] = jnp.zeros_like(acc)
+        acc[...] = jnp.zeros(acc.shape, F32)
 
         def chunk(k, carry):
             at = pl.ds(pl.multiple_of(k * edges, edges), edges)
@@ -379,12 +348,10 @@
     gradient([hub + j * own for j in range(count * CAP // own)], lambda k: None)
     for c in range(4):
         far_lin[pl.ds(c, count * CAP, stride=4), :] = acc[:, cols(c)]
-    greeted(doms, works)
-
-    def far_rows(p):
+    def far_grads(p):
         return far_lin.at[pl.ds(pl.multiple_of(p * msg, msg), msg), :]
 
-    pltpu.make_async_copy(far_rows(me), back.at[me], far_recv).start()
+    pltpu.make_async_copy(far_grads(me), back.at[me], back_recv).start()
     share = count // (4 * steps)
 
     def give(from_step):
@@ -395,7 +362,7 @@
                 @pl.when(i > 0)
                 def _():
                     pd, pw = ring(dom, i // works, doms), ring(work, lax.rem(i, works), works)
-                    send(far_rows(pd * works + pw), back.at[me], far_send, far_recv, (pd, pw))
+                    send(far_grads(pd * works + pw), back.at[me], back_send, back_recv, (pd, pw))
 
         return some
 
@@ -403,17 +370,17 @@
         return [pl.multiple_of((y * 2 + of) * own, own) for y in range(lines)]
 
     gradient(starts(1 - core), give(0))
-    theirs[...] = acc[...].reshape(lines, own, width)
+    theirs[...] = acc[...]
     for y in range(lines):
-        send(theirs.at[y], xbuf.at[y], x_send, x_recv.at[y], (dom, line * 2 + 1 - core))
+        send(theirs.at[pl.ds(y * own, own), :], xbuf.at[y], y_send, y_recv.at[y], (dom, line * 2 + 1 - core))
     gradient(starts(core), give(2 * steps))
 
     for y in range(lines):
-        arrived(xbuf.at[y], x_recv.at[y])
-        mine[y] = acc[y * own:(y + 1) * own, :] + xbuf[y]
+        arrived(xbuf.at[y], y_recv.at[y])
+        mine[pl.ds(y * own, own), :] = acc[pl.ds(y * own, own), :] + xbuf[y]
 
     def piece(y, d):
-        return mine.at[y, pl.ds(pl.multiple_of(d * part, part), part), :]
+        return mine.at[pl.ds(pl.multiple_of(y * own + d * eighth, eighth), eighth), :]
 
     slot = dom * lines + line
     pltpu.make_async_copy(piece(line, dom), r2.at[slot], r2_recv).start()
@@ -426,8 +393,7 @@
     lax.fori_loop(1, doms * lines, scatter, 0)
 
     want_t[...] = want_ref[:, 0, :].T
-    arrived(back, far_recv)
-    lane = lax.rem(me, 128 // CAP) * CAP
+    arrived(back, back_recv)
     row = lax.broadcasted_iota(jnp.int32, (own, count), 0)
     flat = back.reshape(count * msg, 128)
     sums = [jnp.zeros((own, 128), F32) for _ in range(4)]
@@ -449,7 +415,7 @@
 
     lax.fori_loop(1, doms, hand, 0)
     arrived(r3, r3_recv)
-    owner = dom == part_ref[0]
+    owner = dom == hub_ref[0]
     hub_sum = r3[...].reshape(own, width)
     grads = [acc[0:own, cols(k)] + jnp.where(owner, hub_sum[:, cols(k)], 0.0) for k in range(4)]
     square = sum(g * g for g in grads)
@@ -461,73 +427,87 @@
         rows_out[:, cols(k)] = ent_ref[:, cols(k)] - g * scale
     state_out[...] = new.T[0:1, :]
 
-    arrived(xbuf, x_send)
-    arrived(back.at[pl.ds(0, count - 1)], far_send)
+    arrived(xbuf, y_send)
+    arrived(back.at[pl.ds(0, count - 1)], back_send)
     arrived(r2.at[pl.ds(0, doms * lines - 1)], r2_send)
     arrived(r3.at[pl.ds(0, doms - 1)], r3_send)
-
-
-def train(doms, works, w_rows, rel_rows, source, target, negative, wanted, hub_part, entity_rows, state,
-          edges=512):
+    arrived(swapped, x_send)
+    arrived(w_ref.at[pl.ds(0, 2 * (doms * lines - 1) * part)], h2_send)
+    arrived(hub1.at[:, pl.ds(0, doms - 1)], h1_send)
+    arrived(out_buf.at[pl.ds(0, count - 1)], far_send)
+    arrived(want_ref.at[pl.ds(0, count - 1)], req_send)
+
+
+def window(doms, works, entity_rows, state, relations, hub_part, requests, source, relation_ids, target, negative,
+           edges=512):
     own, width = entity_rows.shape
     count = doms * works
     lines = works // 2
-    part = own // doms
-    slots = w_rows.shape[0]
+    part = own // 2 // doms
+    eighth = own // doms
+    slots = works * own + count * CAP
     total = source.size
-    vmem, smem = pl.BlockSpec(memory_space=pltpu.VMEM), pl.BlockSpec(memory_space=pltpu.SMEM)
+    any_, smem = pl.BlockSpec(memory_space=pl.ANY), pl.BlockSpec(memory_space=pltpu.SMEM)
+    vmem = pl.BlockSpec(memory_space=pltpu.VMEM)
     dma = pltpu.SemaphoreType.DMA
+    i32 = jnp.int32
     return pl.pallas_call(
-        functools.partial(train_kernel, doms, works),
-        in_specs=[smem] * 3 + [vmem] * 8,
+        functools.partial(window_kernel, doms, works, edges),
+        in_specs=[smem] * 4 + [any_] * 7,
         out_specs=[vmem, vmem],
         out_shape=[
             jax.ShapeDtypeStruct((own, width), F32),
             jax.ShapeDtypeStruct((1, own), F32),
         ],
         scratch_shapes=[
+            pltpu.VMEM((own, width), F32),
+            pltpu.VMEM(requests.shape, i32),
+            pltpu.VMEM(source.shape, i32),
+            pltpu.VMEM(target.shape, i32),
+            pltpu.VMEM(negative.shape, i32),
+            pltpu.VMEM(state.shape, F32),
+            pltpu.VMEM((slots, 4, 128), F32),
+            pltpu.VMEM((count, 1, 128), i32),
+            pltpu.VMEM((total, width), F32),
+            pltpu.VMEM((own, 4, 128), F32),
+            pltpu.VMEM((2, doms, part, 4, 128), F32),
+            pltpu.VMEM((2, part, 4, 128), F32),
+            pltpu.VMEM((count, CAP, 4, 128), F32),
+            pltpu.VMEM((count * CAP // 128, 1, 128), i32),
+            pltpu.SMEM((count, 1, 128), i32),
+            pltpu.VMEM(relations.shape, F32),
             pltpu.VMEM((slots, width), BF16),
             pltpu.VMEM((width, slots), BF16),
             pltpu.VMEM((2 * source.shape[0], slots, 128), F32),
-            pltpu.VMEM((2 * total // edges, 1, edges), jnp.int32),
+            pltpu.VMEM((2 * total // edges, 1, edges), i32),
             pltpu.VMEM((slots, 2 * total), BF16),
             pltpu.VMEM((2 * total, width), BF16),
             pltpu.VMEM((2 * total, width), BF16),
             pltpu.VMEM((2 * total, width), BF16),
             pltpu.VMEM((edges * 4, 128), F32),
             pltpu.VMEM((edges * 4, 128), F32),
-            pltpu.VMEM((edges, width), F32),
             pltpu.VMEM((edges, 128), F32),
             pltpu.VMEM((2, width, edges), F32),
-            pltpu.VMEM((lines * own, width), F32),
             pltpu.VMEM((count * CAP * 4, 128), F32),
-            pltpu.VMEM((lines, own, width), F32),
-            pltpu.VMEM((lines, own, width), F32),
             pltpu.VMEM((count, CAP * 4, 128), F32),
             pltpu.VMEM((lines, own, width), F32),
-            pltpu.VMEM((doms * lines, part, width), F32),
-            pltpu.VMEM((part, width), F32),
-            pltpu.VMEM((doms, part, width), F32),
-            pltpu.VMEM((128, count), jnp.int32),
+            pltpu.VMEM((doms * lines, eighth, width), F32),
+            pltpu.VMEM((eighth, width), F32),
+            pltpu.VMEM((doms, eighth, width), F32),
+            pltpu.VMEM((128, count), i32),
+            dma((6,)), dma, dma, dma, dma, dma, dma, dma, dma((2, 3)), dma, dma, dma, dma,
             dma, dma((lines,)), dma, dma, dma, dma, dma, dma,
         ],
         compiler_params=pltpu.CompilerParams(
-            collective_id=1, has_side_effects=True, vmem_limit_bytes=60 * MIB
+            collective_id=0, has_side_effects=True, vmem_limit_bytes=60 * MIB
         ),
-        name="train",
-    )(source, target, hub_part, w_rows, rel_rows, source, target, negative, wanted, entity_rows, state)
-
-
-def per_device(doms, works, entity_rows, adagrad_state, relations, hub_part, requests,
-               source_slot, relation_ids, target_slot, negative_slot):
+        name="window",
+    )(hub_part, relation_ids, source, target, entity_rows, requests, relations, source, target, negative, state)
+
+
+def per_device(doms, works, entity_rows, adagrad_state, *others):
     own = entity_rows.shape[0]
-    w_rows, wanted, rel_rows = fetch(
-        doms, works, entity_rows, requests, hub_part, relation_ids, relations
-    )
-    new_rows, new_state = train(
-        doms, works, w_rows, rel_rows, source_slot, target_slot, negative_slot, wanted, hub_part,
-        entity_rows, adagrad_state.reshape(1, own)
-    )
+    new_rows, new_state = window(doms, works, entity_rows, adagrad_state.reshape(1, own), *others)
     return new_rows, new_state.reshape(own)
 
 

time: 153 us -> 138 us (0.902)
  Pallas kernels: 144 us -> 133 us
  local copies, waits for them, and re-layouts: 7.47 us -> 2.8 us
    pallas_call x2 -> x1, Pallas kernels: 144 us -> 133 us  [window(): pl.pallas_call(functools.partial(window_kernel, doms, works, edges), in_s...]
    unnamed x12 -> x2, local copies, waits for them, and re-layouts: 7.47 us -> 2.8 us
where the time goes in v3:
time: 138 us; the launch traced here: 137 us
  Pallas kernels  133 us (96%)
  local copies, waits for them, and re-layouts  2.8 us (2%)
    pallas_call x1, Pallas kernels, window(): pl.pallas_call(functools.partial(window_kernel, doms, works, edges), in_s...  133 us
    unnamed x2, local copies, waits for them, and re-layouts  2.8 us

profile of v3, /device:TPU:1, one launch (start us, length us, event | category | flops | bytes accessed | tf_op | source)
XLA Modules:
  0.0 137.3 jit_solution(18072171928096170951)
XLA Ops:
  1.3 133.2 %window.1 = (f32[128,512]{1,0:T(8,128)}, f32[1,128]{1,0:T(1,128)}) custom-call(s32[1]{0:T(128)S(6)} %copy.13.hub_ref, s32[2,1024]{1,0:T(2,128)} %ids_ref.1, s32[2,1024]{1,0:T(2,128)} %src_hbm.1, s32[2,1024]{1,0:T(2,128)} %tgt_hbm.1, f32[128,512]{1,0:T(8,128)} %ent_hbm.1, s32[1,512]{1,0:T(1,128)} %req_hbm.1, f32[4096,512]{1,0:T(8,128)} %rel_hbm.1, ...), custom_call_target="tpu_custom_call" | custom-call | tf_op jit(solution)/shard_map/window/pallas_call | solution.py:454
  134.5 1.7 %copy.14 = f32[128,512]{1,0:T(8,128)} copy(f32[128,512]{1,0:T(8,128)} %get-tuple-element.8) | data formatting | bytes 524288
  136.2 1.1 copy.15

commit v4 on v3

--- a/solution.py
+++ b/solution.py
@@ -8,6 +8,8 @@
 
 F32 = jnp.float32
 BF16 = jnp.bfloat16
+F8 = jnp.float8_e4m3fn
+LOW = 1024.0
 NT = (((1,), (1,)), ((), ()))
 MESH = pl.DeviceIdType.MESH
 MIB = 1024 * 1024
@@ -66,7 +68,7 @@
                   src_hbm, tgt_hbm, neg_hbm, state_hbm,
                   rows_out, state_out,
                   ent_ref, req_ref, src_v, tgt_v, neg_ref, state_ref,
-                  w_ref, want_ref, rel_ref, erow, hub1, piece, out_buf, reqv, want_s, relv,
+                  w_ref, want_ref, rel_ref, erow, hub1, out_buf, reqv, want_s, relv,
                   wb, wbt, cnt, slot_v, gt, rneg, rhi, rlo, hlin, tlin, slope_v, dneg,
                   far_lin, back, xbuf, r2, total, r3, want_t,
                   in_sem, rel_sem, req_send, req_recv, loc_sem, h1_send, h1_recv, h2_send, h2_recv,
@@ -126,18 +128,9 @@
         send(reqv.at[(pd * works + pw) // per_row], want_ref.at[me], req_send, req_recv, (pd, pw))
 
     for_peers(dom, work, doms, works, ask)
-    arrived(hub1.at[:, pl.ds(0, doms - 1)], h1_recv)
 
     def rows(s, y, d, n):
         return w_ref.at[pl.ds((y * 2 + core) * own + s * half + d * part, n * part)]
-
-    at = hub_ref[0]
-    for s in range(2):
-        piece[s] = hub1[s, at]
-    for s in range(2):
-        copy = pltpu.make_async_copy(piece.at[s], rows(s, line, dom, 1), loc_sem)
-        copy.start()
-        copy.wait()
 
     def along_x(k):
         return (z * SIDE + ring(x, k, SIDE), work)
@@ -158,6 +151,10 @@
     def landed(s, step, n):
         arrived(w_ref.at[pl.ds(0, (SIDE - 1) * n * part)], h2_recv.at[s, step])
 
+    arrived(hub1.at[:, pl.ds(0, doms - 1)], h1_recv)
+    at = hub_ref[0]
+    for s in range(2):
+        w_ref[pl.ds((line * 2 + core) * own + s * half + dom * part, part)] = hub1[s, at]
     hop([rows(0, line, dom, 1)], 0, 0, along_x)
     hop([rows(1, line, dom, 1)], 1, 0, along_y)
 
@@ -232,28 +229,43 @@
 
     swapped = w_ref.at[pl.ds(0, hub // 2)]
     arrived(swapped, x_recv)
+
+    def narrow(first, end):
+        for c in range(4):
+            column = w_ref[first:end, c, :]
+            wb[first:end, cols(c)] = column.astype(BF16)
+            wbt[cols(c), first:end] = column.T.astype(BF16)
+
+    narrow(0, hub)
     arrived(w_ref.at[pl.ds(hub, count * CAP)], far_recv)
-    for c in range(4):
-        column = w_ref[:, c, :]
-        wb[:, cols(c)] = column.astype(BF16)
-        wbt[cols(c), :] = column.T.astype(BF16)
+
+    narrow(hub, slots)
 
     block = 128
     eighth = own // doms
     msg = CAP * 4
     acc, theirs, mine, qf = (relv.at[pl.ds(k * lines * own, lines * own), :] for k in range(4))
 
+    def gather(i, at, n):
+        b, first = i // tiles, lax.rem(i, tiles) * edges + at
+        place = (lax.rem(i, 2) * edges + at) * 4
+        for e in range(n):
+            to = pl.ds(pl.multiple_of(place + e * 4, 4), 4)
+            hlin[to, :] = w_ref[source_s[b, first + e]]
+            tlin[to, :] = w_ref[target_s[b, first + e]]
+
+    def gather_first(k, carry):
+        gather(0, k * 16, 16)
+        return carry
+
+    lax.fori_loop(0, edges // 16, gather_first, 0)
+
     def step(i, carry):
-        b, first = i // tiles, lax.rem(i, tiles) * edges
+        b = i // tiles
         base = i * edges
-
-        def gather(e, carry):
-            at = pl.ds(pl.multiple_of(e * 4, 4), 4)
-            hlin[at, :] = w_ref[source_s[b, first + e]]
-            tlin[at, :] = w_ref[target_s[b, first + e]]
-            return carry
-
-        lax.fori_loop(0, edges, gather, 0, unroll=8)
+        coming = lax.rem(i + 1, steps)
+
+        held = lax.rem(i, 2) * edges
 
         def forward(k, carry):
             row = pl.multiple_of(k * block, block)
@@ -264,8 +276,8 @@
             score = jnp.zeros((block, 128), F32)
             for p in range(2):
                 q = p + 2
-                hr, hi = (hlin[pl.ds(4 * row + c, block, stride=4), :] for c in (p, q))
-                tr, ti = (tlin[pl.ds(4 * row + c, block, stride=4), :] for c in (p, q))
+                hr, hi = (hlin[pl.ds(4 * (held + row) + c, block, stride=4), :] for c in (p, q))
+                tr, ti = (tlin[pl.ds(4 * (held + row) + c, block, stride=4), :] for c in (p, q))
                 rr, ri = rel_ref[there, cols(p)], rel_ref[there, cols(q)]
                 qr = hr * rr - hi * ri
                 qi = hr * ri + hi * rr
@@ -282,15 +294,23 @@
 
         lax.fori_loop(0, edges // block, forward, 0)
 
-        for side in range(2):
+        def score(side, carry):
             there = pl.ds(pl.multiple_of(2 * base + side * edges, edges), edges)
-            for m in range(slots // 512):
+            parts = slots // 512
+            few = edges // 2 // (parts + 1)
+            for m in range(parts):
                 rows = slice(m * 512, (m + 1) * 512)
                 st = lax.dot_general(wb[rows, :], rneg[there, :], NT, preferred_element_type=F32)
+                gather(coming, side * (edges // 2) + m * few, few)
                 weight = cnt[b * 2 + 1 - side, rows, :]
                 weight = jnp.concatenate([weight] * (edges // 128), axis=1)
                 gt[rows, there] = (weight * jnp.tanh(0.5 * st) + weight).astype(BF16)
+            gather(coming, side * (edges // 2) + parts * few, few)
             dneg[side] = jnp.dot(wbt[...], gt[:, there], preferred_element_type=F32)
+            return carry
+
+        score(0, 0)
+        score(1, 0)
 
         def backward(k, carry):
             row = pl.multiple_of(k * block, block)
@@ -302,13 +322,13 @@
             def put(at, c, value):
                 top = value.astype(BF16)
                 rhi[at, cols(c)] = top
-                rlo[at, cols(c)] = (value - top.astype(F32)).astype(BF16)
+                rlo[at, cols(c)] = ((value - top.astype(F32)) * LOW).astype(F8)
 
             slope = slope_v[here, :]
             for p in range(2):
                 q = p + 2
                 rr, ri = rel_ref[there, cols(p)], rel_ref[there, cols(q)]
-                tr, ti = (tlin[pl.ds(4 * row + c, block, stride=4), :] for c in (p, q))
+                tr, ti = (tlin[pl.ds(4 * (held + row) + c, block, stride=4), :] for c in (p, q))
                 dqr = slope * tr + dneg[0, cols(p), here].T
                 dqi = slope * ti + dneg[0, cols(q), here].T
                 put(source, p, dqr * rr + dqi * ri)
@@ -335,10 +355,11 @@
                 [(number == slot - start).astype(F32).astype(BF16) for start in starts], axis=0
             )
             weight = jnp.concatenate([gt[pl.ds(start, own), at] for start in starts], axis=0)
+            low = jnp.dot(hot.astype(F8), rlo[at, :], preferred_element_type=F32)
             acc[...] += (
                 jnp.dot(weight, rneg[at, :], preferred_element_type=F32)
                 + jnp.dot(hot, rhi[at, :], preferred_element_type=F32)
-                + jnp.dot(hot, rlo[at, :], preferred_element_type=F32)
+                + low * (1.0 / LOW)
             )
             beside(k)
             return carry
@@ -471,7 +492,6 @@
             pltpu.VMEM((total, width), F32),
             pltpu.VMEM((own, 4, 128), F32),
             pltpu.VMEM((2, doms, part, 4, 128), F32),
-            pltpu.VMEM((2, part, 4, 128), F32),
             pltpu.VMEM((count, CAP, 4, 128), F32),
             pltpu.VMEM((count * CAP // 128, 1, 128), i32),
             pltpu.SMEM((count, 1, 128), i32),
@@ -483,9 +503,9 @@
             pltpu.VMEM((slots, 2 * total), BF16),
             pltpu.VMEM((2 * total, width), BF16),
             pltpu.VMEM((2 * total, width), BF16),
-            pltpu.VMEM((2 * total, width), BF16),
-            pltpu.VMEM((edges * 4, 128), F32),
-            pltpu.VMEM((edges * 4, 128), F32),
+            pltpu.VMEM((2 * total, width), F8),
+            pltpu.VMEM((2 * edges * 4, 128), F32),
+            pltpu.VMEM((2 * edges * 4, 128), F32),
             pltpu.VMEM((edges, 128), F32),
             pltpu.VMEM((2, width, edges), F32),
             pltpu.VMEM((count * CAP * 4, 128), F32),

time: 138 us -> 131 us (0.949)
  Pallas kernels: 133 us -> 126 us
    pallas_call x1, Pallas kernels: 133 us -> 126 us  [window(): pl.pallas_call(functools.partial(window_kernel, doms, works, edges), in_s...]
where the time goes in v4:
time: 131 us; the launch traced here: 130 us
  Pallas kernels  126 us (96%)
  local copies, waits for them, and re-layouts  2.8 us (2%)
    pallas_call x1, Pallas kernels, window(): pl.pallas_call(functools.partial(window_kernel, doms, works, edges), in_s...  126 us
    unnamed x2, local copies, waits for them, and re-layouts  2.8 us

profile of v4, /device:TPU:1, one launch (start us, length us, event | category | flops | bytes accessed | tf_op | source)
XLA Modules:
  0.0 130.3 jit_solution(9169313113025475348)
XLA Ops:
  1.3 126.2 %window.1 = (f32[128,512]{1,0:T(8,128)}, f32[1,128]{1,0:T(1,128)}) custom-call(s32[1]{0:T(128)S(6)} %copy.13.hub_ref, s32[2,1024]{1,0:T(2,128)} %ids_ref.1, s32[2,1024]{1,0:T(2,128)} %src_hbm.1, s32[2,1024]{1,0:T(2,128)} %tgt_hbm.1, f32[128,512]{1,0:T(8,128)} %ent_hbm.1, s32[1,512]{1,0:T(1,128)} %req_hbm.1, f32[4096,512]{1,0:T(8,128)} %rel_hbm.1, ...), custom_call_target="tpu_custom_call" | custom-call | tf_op jit(solution)/shard_map/window/pallas_call | solution.py:475
  127.5 1.7 %copy.14 = f32[128,512]{1,0:T(8,128)} copy(f32[128,512]{1,0:T(8,128)} %get-tuple-element.8) | data formatting | bytes 524288
  129.2 1.1 copy.15

commit v5 on v4

--- a/solution.py
+++ b/solution.py
@@ -267,8 +267,8 @@
 
         held = lax.rem(i, 2) * edges
 
-        def forward(k, carry):
-            row = pl.multiple_of(k * block, block)
+        def forward(k):
+            row = k * block
             here = pl.ds(row, block)
             there = pl.ds(pl.multiple_of(base + row, block), block)
             query = pl.ds(pl.multiple_of(2 * base + row, block), block)
@@ -290,9 +290,9 @@
                 rneg[mirror, cols(q)] = (rr * ti - ri * tr).astype(BF16)
             positive = jnp.sum(score, axis=1, keepdims=True)
             slope_v[here, :] = jnp.broadcast_to(0.5 * jnp.tanh(0.5 * positive) - 0.5, (block, 128))
-            return carry
-
-        lax.fori_loop(0, edges // block, forward, 0)
+
+        for k in range(edges // block):
+            forward(k)
 
         def score(side, carry):
             there = pl.ds(pl.multiple_of(2 * base + side * edges, edges), edges)
@@ -373,28 +373,34 @@
         return far_lin.at[pl.ds(pl.multiple_of(p * msg, msg), msg), :]
 
     pltpu.make_async_copy(far_grads(me), back.at[me], back_recv).start()
-    share = count // (4 * steps)
-
-    def give(from_step):
-        def some(k):
-            for n in range(share):
-                i = (from_step + k) * share + n
-
-                @pl.when(i > 0)
-                def _():
-                    pd, pw = ring(dom, i // works, doms), ring(work, lax.rem(i, works), works)
-                    send(far_grads(pd * works + pw), back.at[me], back_send, back_recv, (pd, pw))
-
-        return some
+    loops = 2 * steps
+
+    def give(pd, pw):
+        send(far_grads(pd * works + pw), back.at[me], back_send, back_recv, (pd, pw))
+
+    def give_group(k):
+        for pw in near:
+            give(ring(dom, k + 1, doms), pw)
+
+    share = (doms - 1 - loops) * works // loops
+
+    def give_share(k):
+        for n in range(share):
+            i = k * share + n
+            give(ring(dom, loops + 1 + i // works, doms), ring(work, lax.rem(i, works), works))
+
+    near = [ring(work, k, works) for k in range(works)]
+    for pw in near[1:]:
+        give(dom, pw)
 
     def starts(of):
         return [pl.multiple_of((y * 2 + of) * own, own) for y in range(lines)]
 
-    gradient(starts(1 - core), give(0))
+    gradient(starts(1 - core), give_group)
     theirs[...] = acc[...]
     for y in range(lines):
         send(theirs.at[pl.ds(y * own, own), :], xbuf.at[y], y_send, y_recv.at[y], (dom, line * 2 + 1 - core))
-    gradient(starts(core), give(2 * steps))
+    gradient(starts(core), give_share)
 
     for y in range(lines):
         arrived(xbuf.at[y], y_recv.at[y])
@@ -406,12 +412,20 @@
     slot = dom * lines + line
     pltpu.make_async_copy(piece(line, dom), r2.at[slot], r2_recv).start()
 
-    def scatter(i, carry):
-        pd, py = ring(dom, i // lines, doms), ring(line, lax.rem(i, lines), lines)
+    spots = [ring(line, k, lines) for k in range(lines)]
+
+    def scatter(pd, py):
         send(piece(py, pd), r2.at[slot], r2_send, r2_recv, (pd, py * 2 + core))
+
+    for py in spots[1:]:
+        scatter(dom, py)
+
+    def scatter_along(i, carry):
+        for py in spots:
+            scatter(ring(dom, i, doms), py)
         return carry
 
-    lax.fori_loop(1, doms * lines, scatter, 0)
+    lax.fori_loop(1, doms, scatter_along, 0)
 
     want_t[...] = want_ref[:, 0, :].T
     arrived(back, back_recv)

time: 131 us -> 128 us (0.977)
  Pallas kernels: 126 us -> 123 us
    pallas_call x1, Pallas kernels: 126 us -> 123 us  [window(): pl.pallas_call(functools.partial(window_kernel, doms, works, edges), in_s...]
where the time goes in v5:
time: 128 us
  Pallas kernels  123 us (96%)
  local copies, waits for them, and re-layouts  2.8 us (2%)
  between operations  1.29 us (1%)
    pallas_call x1, Pallas kernels, window(): pl.pallas_call(functools.partial(window_kernel, doms, works, edges), in_s...  123 us
    unnamed x2, local copies, waits for them, and re-layouts  2.8 us

profile of v5, /device:TPU:1, one launch (start us, length us, event | category | flops | bytes accessed | tf_op | source)
XLA Modules:
  0.0 127.5 jit_solution(917355269115131727)
XLA Ops:
  1.3 123.4 %window.1 = (f32[128,512]{1,0:T(8,128)}, f32[1,128]{1,0:T(1,128)}) custom-call(s32[1]{0:T(128)S(6)} %copy.13.hub_ref, s32[2,1024]{1,0:T(2,128)} %ids_ref.1, s32[2,1024]{1,0:T(2,128)} %src_hbm.1, s32[2,1024]{1,0:T(2,128)} %tgt_hbm.1, f32[128,512]{1,0:T(8,128)} %ent_hbm.1, s32[1,512]{1,0:T(1,128)} %req_hbm.1, f32[4096,512]{1,0:T(8,128)} %rel_hbm.1, ...), custom_call_target="tpu_custom_call" | custom-call | tf_op jit(solution)/shard_map/window/pallas_call | solution.py:489
  124.7 1.7 %copy.14 = f32[128,512]{1,0:T(8,128)} copy(f32[128,512]{1,0:T(8,128)} %get-tuple-element.8) | data formatting | bytes 524288
  126.4 1.1 copy.15
